TPU v7x, 256 devices: a whole 4x4x8 slice. The times are simulated.
256 devices in a mesh: row: 16 (over y, x), col: 16 (over z, core).
Axes of the slice: x: 4, y: 4, z: 8, core: 2. Of those that a mesh axis runs over, the one named last changes fastest.
Arguments:
- kernel: float32 [20480, 20480], P('row', 'col'), may hold values from 0 to 3, as said below
- noise: float32 [20480], P('row'), may hold values from 0.3 to 1
Outputs:
- factored: float32 [20480, 20480], P('row', 'col')
Inputs may be any that keep to these rules, and one draw needn't show every extreme that they name: In global order kernel is symmetric and positive semidefinite, and all its entries are positive.
All inputs are finite; a program needn't handle non-finite values.
Results may differ from a plain program's by a relative error of at most 0.0001.
Values sent between devices are 32-bit elements; how exact they have to be, the bound alone decides.
A program may use at most 128 MiB of HBM per device.

v0:
```python
import jax
import jax.numpy as jnp
from jax import lax
from jax.sharding import PartitionSpec as P

NB = 256


def broadcast(block, axis, source):
    block = jnp.where(lax.axis_index(axis) == source, block, jnp.zeros_like(block))
    return lax.psum(block, axis)


def factor_block(block):
    whole = jnp.tril(block) + jnp.tril(block, -1).T
    factor = jnp.linalg.cholesky(whole)
    eye = jnp.eye(block.shape[0], dtype=block.dtype)
    inverse = lax.linalg.triangular_solve(factor, eye, left_side=True, lower=True)
    return (factor, inverse)


def solve_rows(rows_in, inverse):
    return jnp.dot(
        rows_in, inverse.T, precision=lax.Precision.HIGHEST, preferred_element_type=jnp.float32
    )


def pick_rows(row_rows, n_row, n_col, col_index, col_count):
    groups = n_col // n_row
    shaped = row_rows.reshape(col_count, groups, NB, NB)
    chosen = lax.dynamic_index_in_dim(shaped, col_index // n_row, 1, keepdims=False)
    return chosen.reshape(col_count * NB, NB)


def panel_data(k, slab, n_row, n_col, col_index, col_count):
    diag_tile = broadcast(slab[:NB], "row", k % n_row)
    factor, inverse = factor_block(diag_tile)
    solved = solve_rows(slab, inverse)
    row_panel = broadcast(solved, "col", k)
    col_panel = broadcast(
        pick_rows(row_panel, n_row, n_col, col_index, col_count), "row", col_index % n_row
    )
    return (factor, row_panel, col_panel)


def advance(k, part, part_cols, row_block, col_index, row_panel, col_panel, factor):
    product = jnp.einsum(
        "rk,ck->rc",
        row_panel,
        col_panel,
        precision=lax.Precision.HIGHEST,
        preferred_element_type=jnp.float32,
    )
    touch = (row_block[:, None] >= part_cols[None, :]) & (part_cols[None, :] > k)
    part = jnp.where(touch, part - product, part)
    slab = part[:, :NB]
    owner = col_index == k
    slab = jnp.where((row_block > k)[:, None] & owner, row_panel, slab)
    factor_rows = jnp.tile(factor, (part.shape[0] // NB, 1))
    slab = jnp.where((row_block == k)[:, None] & owner, factor_rows, slab)
    part = jnp.concatenate([slab, part[:, NB:]], axis=1)
    return part


def body(kernel, noise):
    n_row = lax.axis_size("row")
    n_col = lax.axis_size("col")
    row_index = lax.axis_index("row")
    col_index = lax.axis_index("col")
    rows_local, cols_local = kernel.shape
    col_count = cols_local // NB
    row_iota = lax.iota(jnp.int32, rows_local)
    col_iota = lax.iota(jnp.int32, cols_local)
    row_block = row_iota // NB * n_row + row_index
    col_block = col_iota // NB * n_col + col_index
    row_elem = row_block * NB + row_iota % NB
    col_elem = col_block * NB + col_iota % NB
    matrix = kernel + jnp.where(row_elem[:, None] == col_elem[None, :], noise[:, None], 0.0)
    for k in range(2):
        factor, row_panel, col_panel = panel_data(
            k, matrix[:, :NB], n_row, n_col, col_index, col_count
        )
        matrix = advance(k, matrix, col_block, row_block, col_index, row_panel, col_panel, factor)
    return matrix


def solution(mesh):
    return jax.shard_map(
        body,
        mesh=mesh,
        in_specs=(P("row", "col"), P("row")),
        out_specs=P("row", "col"),
        check_vma=False,
    )
```

profile of v0, /device:TPU:141, one launch (start us, length us, event | category | flops | bytes accessed | tf_op | source)
XLA Modules:
  0.0 795.0 jit_solution(16474102595706877903)
XLA Ops:
  6.5 3.6 select_add_fusion
  10.1 2.8 copy-done
  12.9 0.7 slice_select_fusion.3
  13.8 92.1 %all-reduce.8.cloned.1.call-done = f32[256,256]{1,0:T(8,128)} async-done(((f32[256,256]{1,0:T(8,128)}), f32[256,256]{1,0:T(8,128)}) %all-reduce.8.cloned.1.call-update) | async-done | bytes 262160 | tf_op jit(solution)/shard_map/psum | solution.py:11
  105.9 1.1 copy.3
  107.0 1.0 bitcast_add_fusion.3
  108.2 11.7 %cholesky.130 = f32[128,128]{1,0:T(8,128)S(1)} custom-call(f32[128,128]{1,0:T(8,128)S(1)} %cholesky.194), custom_call_target="Cholesky" | custom-call | tf_op jit(solution)/shard_map/jit(cholesky)/cholesky | solution.py:16
  120.0 9.8 %custom-call.13 = f32[1,128,128]{1,2,0:T(8,128)S(1)} custom-call(f32[1,128,128]{2,1,0:T(8,128)S(1)} %get-tuple-element.54), custom_call_target="InvertDiagBlocksLowerTriangular" | custom-call | tf_op jit(solution)/shard_map/jit(cholesky)/cholesky | solution.py:16
  130.3 11.7 %cholesky.147 = f32[128,128]{1,0:T(8,128)S(1)} custom-call(f32[128,128]{1,0:T(8,128)S(1)} %convolution_subtract_fusion.5), custom_call_target="Cholesky" | custom-call | tf_op jit(solution)/shard_map/jit(cholesky)/cholesky | solution.py:16
  142.0 0.6 compare_reduce_fusion.2
  142.7 0.7 compare_reduce_fusion.3
  144.8 4.5 while.4
  145.2 0.7 fusion.67
  145.9 1.3 bitcast_dynamic-update-slice_fusion.4
  147.3 0.7 fusion.67
  147.9 1.3 bitcast_dynamic-update-slice_fusion.4
  149.3 19.7 %custom-call.14 = f32[2,128,128]{1,2,0:T(8,128)S(1)} custom-call(f32[2,128,128]{2,1,0:T(8,128)S(1)} %get-tuple-element.21), custom_call_target="InvertDiagBlocksLowerTriangular" | custom-call | tf_op jit(solution)/shard_map/triangular_solve/custom-call.0 | solution.py:18
  169.9 3.6 convolution_select_fusion.1
  173.6 112.9 %all-reduce.10.cloned.1.call-done = f32[1280,256]{1,0:T(8,128)} async-done(((f32[1280,256]{1,0:T(8,128)}), f32[1280,256]{1,0:T(8,128)}) %all-reduce.10.cloned.1.call-update) | async-done | bytes 1310736 | tf_op jit(solution)/shard_map/psum | solution.py:11
  286.5 1.2 broadcast_select_fusion.1
  287.8 100.4 %all-reduce.12.cloned.1.call-done = f32[1280,256]{1,0:T(8,128)} async-done(((f32[1280,256]{1,0:T(8,128)}), f32[1280,256]{1,0:T(8,128)}) %all-reduce.12.cloned.1.call-update) | async-done | bytes 1310736 | tf_op jit(solution)/shard_map/psum | solution.py:11
  388.2 8.8 %fusion.1 = f32[1280,1280]{1,0:T(8,128)S(1)} fusion(f32[1280,1280]{1,0:T(8,128)} %copy-done, f32[1280,256]{1,0:T(8,128)S(1)} %copy-done.2, f32[1280,256]{1,0:T(8,128)} %all-reduce.12.cloned.1.call-done, s32[1280]{0:T(1024)S(1)} %fusion.45, s32[1280]{0:T(1024)S(1)} %fusion.46, pred[1280]{0:T(1024)(128)(4,1)S(1)} %broadcast_compare_fusion), kind=kOutput, calls=%fused_computation.7 | convolution fusion | flops 5039718400 | bytes 15740160 | tf_op jit(solution)/shard_map/rk,ck->rc/dot_general | solution.py:47
  397.0 2.8 copy-done.1
  399.8 0.4 fusion.3
  400.2 0.7 slice_select_fusion.2
  401.3 92.9 %all-reduce.14.cloned.1.call-done = f32[256,256]{1,0:T(8,128)} async-done(((f32[256,256]{1,0:T(8,128)}), f32[256,256]{1,0:T(8,128)}) %all-reduce.14.cloned.1.call-update) | async-done | bytes 262160 | tf_op jit(solution)/shard_map/psum | solution.py:11
  494.2 1.0 broadcast_select_fusion.2
  495.3 1.0 bitcast_add_fusion.1
  496.6 11.7 %cholesky.164 = f32[128,128]{1,0:T(8,128)S(1)} custom-call(f32[128,128]{1,0:T(8,128)S(1)} %cholesky.197), custom_call_target="Cholesky" | custom-call | tf_op jit(solution)/shard_map/jit(cholesky)/cholesky | solution.py:16
  508.3 9.8 %custom-call.15 = f32[1,128,128]{1,2,0:T(8,128)S(1)} custom-call(f32[1,128,128]{2,1,0:T(8,128)S(1)} %get-tuple-element.50), custom_call_target="InvertDiagBlocksLowerTriangular" | custom-call | tf_op jit(solution)/shard_map/jit(cholesky)/cholesky | solution.py:16
  518.6 11.7 %cholesky.181 = f32[128,128]{1,0:T(8,128)S(1)} custom-call(f32[128,128]{1,0:T(8,128)S(1)} %convolution_subtract_fusion.4), custom_call_target="Cholesky" | custom-call | tf_op jit(solution)/shard_map/jit(cholesky)/cholesky | solution.py:16
  530.4 0.6 compare_reduce_fusion
  531.0 0.7 compare_reduce_fusion.1
  533.1 4.3 while.5
  533.3 0.7 fusion.68
  534.0 1.3 bitcast_dynamic-update-slice_fusion.5
  535.3 0.7 fusion.68
  536.0 1.3 bitcast_dynamic-update-slice_fusion.5
  537.3 19.7 %custom-call.16 = f32[2,128,128]{1,2,0:T(8,128)S(1)} custom-call(f32[2,128,128]{2,1,0:T(8,128)S(1)} %get-tuple-element.22), custom_call_target="InvertDiagBlocksLowerTriangular" | custom-call | tf_op jit(solution)/shard_map/triangular_solve/custom-call.0 | solution.py:18
  557.9 2.3 convolution_select_fusion
  560.3 112.7 %all-reduce.16.cloned.1.call-done = f32[1280,256]{1,0:T(8,128)} async-done(((f32[1280,256]{1,0:T(8,128)}), f32[1280,256]{1,0:T(8,128)}) %all-reduce.16.cloned.1.call-update) | async-done | bytes 1310736 | tf_op jit(solution)/shard_map/psum | solution.py:11
  673.0 1.3 broadcast_select_fusion
  674.4 5.8 slice.107
  680.1 94.1 %all-reduce.18.cloned.1.call-done = f32[1280,256]{1,0:T(8,128)} async-done(((f32[1280,256]{1,0:T(8,128)}), f32[1280,256]{1,0:T(8,128)}) %all-reduce.18.cloned.1.call-update) | async-done | bytes 1310736 | tf_op jit(solution)/shard_map/psum | solution.py:11
  774.3 9.1 %fusion = f32[1280,1280]{1,0:T(8,128)S(1)} fusion(f32[1280,256]{1,0:T(8,128)S(1)} %copy-done.3, f32[1280,256]{1,0:T(8,128)} %all-reduce.18.cloned.1.call-done, f32[1280,1024]{1,0:T(8,128)} %slice.107, f32[1280,256]{1,0:T(8,128)S(1)} %fusion.3, s32[1280]{0:T(1024)S(1)} %fusion.45, s32[1280]{0:T(1024)S(1)} %fusion.46, ...), kind=kOutput, calls=%fused_computation.5 | convolution fusion | flops 5041356800 | bytes 15740160 | tf_op jit(solution)/shard_map/rk,ck->rc/dot_general | solution.py:47
  783.3 0.6 slice.109
  784.0 0.5 fusion.2
  784.5 3.4 pad_maximum_fusion
  (62 shorter events, 4.3 us)
Async XLA Ops:
  6.5 99.3 %all-reduce.8.cloned.1.call-start = ((), (), s32[]{:S(2)}) async-start(), calls=%async_computation | async-start | bytes 524288 | tf_op jit(solution)/shard_map/psum | solution.py:11
  10.1 2.8 copy-start
  13.7 272.8 %all-reduce.10.cloned.1.call-start = ((), (), s32[]{:S(2)}) async-start(), calls=%async_computation.1 | async-start | bytes 2621440 | tf_op jit(solution)/shard_map/psum | solution.py:11
  173.5 214.6 %all-reduce.12.cloned.1.call-start = ((), (), s32[]{:S(2)}) async-start(), calls=%async_computation.2 | async-start | bytes 2621440 | tf_op jit(solution)/shard_map/psum | solution.py:11
  287.6 100.5 %copy-start.2 = (f32[1280,256]{1,0:T(8,128)S(1)}, f32[1280,256]{1,0:T(8,128)}, u32[]{:S(2)}) copy-start(f32[1280,256]{1,0:T(8,128)} %all-reduce.10.cloned.1.call-done) | copy-start | bytes 3932164
  287.7 206.5 %all-reduce.14.cloned.1.call-start = ((), (), s32[]{:S(2)}) async-start(), calls=%async_computation.3 | async-start | bytes 524288 | tf_op jit(solution)/shard_map/psum | solution.py:11
  397.0 2.8 copy-start.1
  400.9 272.1 %all-reduce.16.cloned.1.call-start = ((), (), s32[]{:S(2)}) async-start(), calls=%async_computation.4 | async-start | bytes 2621440 | tf_op jit(solution)/shard_map/psum | solution.py:11
  560.3 214.0 %all-reduce.18.cloned.1.call-start = ((), (), s32[]{:S(2)}) async-start(), calls=%async_computation.5 | async-start | bytes 2621440 | tf_op jit(solution)/shard_map/psum | solution.py:11
  674.4 99.9 %copy-start.3 = (f32[1280,256]{1,0:T(8,128)S(1)}, f32[1280,256]{1,0:T(8,128)}, u32[]{:S(2)}) copy-start(f32[1280,256]{1,0:T(8,128)} %all-reduce.16.cloned.1.call-done) | copy-start | bytes 3932164
Sparse Core Ops, SparseCore 0:
  13.8 92.0 all-reduce.7
  173.7 112.7 all-reduce.9
  290.1 98.0 all-reduce.11
  401.0 93.1 all-reduce.13
  560.4 112.6 all-reduce.15
  676.2 98.0 all-reduce.17
where the time goes:
time: 808 us; the launch traced here: 795 us
  waiting for transfers between devices  605 us (75%)
  other arithmetic  124 us (15%)
  matrix products  26.5 us (3%)
  local copies, waits for them, and re-layouts  21.8 us (3%)
  between operations  16.6 us (2%)
    psum x6, waiting for transfers between devices, broadcast(): return lax.psum(block, axis)  605 us
    another operation x14, other arithmetic, factor_block(): factor = jnp.linalg.cholesky(whole)  69.3 us
    another operation x5, other arithmetic, factor_block(): lax.linalg.triangular_solve(factor, eye, left_side=True, lower=True)  39.4 us
    dot_general x2, matrix products, advance(): jnp.einsum('rk,ck->rc', row_panel, col_panel, precision=lax.Precision.HIG...  17.9 us
  transfers between devices with their start and end apart: 6, of which 6 were waited for; matrix products, arithmetic and copies ran while one was open for 1% of the time, Pallas kernels for 0%

commit v1 on v0

v1 whole, which is shorter than its diff:
```python
import functools

import jax
import jax.numpy as jnp
from jax import lax
from jax.experimental import pallas as pl
from jax.experimental.pallas import tpu as pltpu
from jax.sharding import PartitionSpec as P

NB = 256
T = 5
LOCAL = NB * T
MESH = pl.DeviceIdType.MESH
HIGHEST = lax.Precision.HIGHEST
HIGH = lax.Precision.HIGH
F32 = jnp.float32

NA = 20
A_ROWS = LOCAL // NA
NBC = 16
B_ROWS = NB // NBC
NF = 6
F_ROWS = NB * 3 // NF


def dot(a, b, dims, precision=HIGHEST):
    return lax.dot_general(a, b, (dims, ((), ())), precision=precision, preferred_element_type=F32)


def nn(a, b, precision=HIGHEST):
    return dot(a, b, ((1,), (0,)), precision)


def nt(a, b, precision=HIGHEST):
    return dot(a, b, ((1,), (1,)), precision)


def tn(a, b, precision=HIGHEST):
    return dot(a, b, ((0,), (0,)), precision)


def eliminate(rows, first):
    width = rows.shape[1]
    done = []
    for g in range(4):
        n = rows.shape[0]
        sub = lax.broadcasted_iota(jnp.int32, (n, 128), 0)
        at = first + 8 * g
        cols = [jnp.broadcast_to(rows[:, at + c : at + c + 1], (n, 128)) for c in range(8)]
        for j in range(8):
            inv = pltpu.reciprocal(cols[j][j : j + 1, :], approx=True)
            scale = jnp.where(sub > j, cols[j] * inv, 0.0)
            for c in range(j + 1, 8):
                cols[c] = cols[c] - scale * cols[c][j : j + 1, :]
            pivot = rows[j : j + 1, :]
            rows = jnp.concatenate(
                [rows[:, w : w + 128] - scale * pivot[:, w : w + 128] for w in range(0, width, 128)], axis=1
            )
        sub8 = lax.broadcasted_iota(jnp.int32, (8, 128), 0)
        diag = cols[0][:8]
        for j in range(1, 8):
            diag = jnp.where(sub8 == j, cols[j][:8], diag)
        root = lax.rsqrt(diag)
        done.append(rows[:8] * jnp.concatenate([root] * (width // 128), axis=1))
        rows = rows[8:]
    return jnp.concatenate(done, axis=0)


def factor_inverse(work):
    following = None
    for k in range(8):
        r0 = 32 * k
        lo, hi = r0 // 128 * 128, NB + (r0 + 32 + 127) // 128 * 128
        rows = work[r0 : r0 + 32, lo:hi] if following is None else following
        rows = eliminate(rows, r0 - lo)
        work[r0 : r0 + 32, lo:hi] = rows
        if k == 7:
            break
        r1 = r0 + 32
        lo1, hi1 = r1 // 128 * 128, NB + (r1 + 32 + 127) // 128 * 128
        product = tn(rows[:, r1 - lo : r1 - lo + 32], rows)
        if hi1 > hi:
            product = jnp.concatenate([product, jnp.zeros((32, hi1 - hi), F32)], axis=1)
        following = work[r1 : r1 + 32, lo1:hi1] - product[:, lo1 - lo :]
        if k < 6:
            r2 = r1 + 32
            lo2 = r2 // 128 * 128
            product = tn(rows[:, lo2 - lo : NB - lo], rows[:, lo2 - lo :])
            work[r2:NB, lo2:hi] = work[r2:NB, lo2:hi] - product[r2 - lo2 :, :]


def identity():
    i0 = lax.broadcasted_iota(jnp.int32, (NB, NB), 0)
    i1 = lax.broadcasted_iota(jnp.int32, (NB, NB), 1)
    return i0 == i1


def gather_kernel(
    kernel_ref, noise_ref, a_out, b_out, f_out,
    a_buf, b_buf, f_buf, m_buf, work,
    a_recv, a_send, s_recv, s_send, b_recv, b_send, f_recv, f_send, m_recv, m_send, local,
):
    p, q = lax.axis_index("row"), lax.axis_index("col")
    y, x, z, c = p // 4, p % 4, q // 2, q % 2
    xp, xm = y * 4 + (x + 1) % 4, y * 4 + (x + 3) % 4
    yp, ym = (y + 1) % 4 * 4 + x, (y + 3) % 4 * 4 + x
    zp, zm = (z + 1) % 8 * 2 + c, (z + 7) % 8 * 2 + c
    sib = z * 2 + 1 - c
    to_xp, to_xm, to_yp, to_ym = (xp, q), (xm, q), (yp, q), (ym, q)
    to_zp, to_zm, to_sib = (p, zp), (p, zm), (p, sib)
    head = (p == 0) & (q == 0)

    a_load = pltpu.make_async_copy(kernel_ref.at[:, pl.ds(0, NB)], a_buf.at[c], local.at[0])
    b_load = pltpu.make_async_copy(kernel_ref.at[pl.ds(0, NB), :], b_buf.at[p % 2], local.at[1])

    @pl.when(z == 0)
    def _():
        a_load.start()

    @pl.when(p < 2)
    def _():
        b_load.start()

    barrier = pltpu.get_barrier_semaphore()
    for device in (to_xp, to_xm, to_yp, to_ym, to_zp, to_zm, to_sib):
        pl.semaphore_signal(barrier, inc=1, device_id=device, device_id_type=MESH)

    @pl.when(head)
    def _():
        pl.semaphore_signal(barrier, inc=1, device_id=(1, 1), device_id_type=MESH)

    @pl.when(z == 0)
    def _():
        a_load.wait()

    @pl.when(p < 2)
    def _():
        b_load.wait()

    @pl.when((z == 0) & (p == c))
    def _():
        a_buf[c, :NB, :] = a_buf[c, :NB, :] + jnp.where(identity(), noise_ref[:, :NB], 0.0)

    pl.semaphore_wait(barrier, jnp.where((p == 1) & (q == 1), 8, 7))

    def m_copy(which):
        return pltpu.make_async_remote_copy(
            src_ref=a_buf.at[which, pl.ds(0, NB), :], dst_ref=m_buf.at[which],
            send_sem=m_send.at[which], recv_sem=m_recv.at[which], device_id=(0, 0), device_id_type=MESH,
        )

    @pl.when((p == 1) & (q == 0))
    def _():
        m_copy(0).start()

    @pl.when((p == 1) & (q == 1))
    def _():
        m_copy(1).start()

    def a_ring(n, device):
        part = a_buf.at[c, pl.ds(n * A_ROWS, A_ROWS), :]
        return pltpu.make_async_remote_copy(
            src_ref=part, dst_ref=part, send_sem=a_send.at[n], recv_sem=a_recv.at[n],
            device_id=device, device_id_type=MESH,
        )

    def a_sib(n, stream):
        part = a_buf.at[stream, pl.ds(n * A_ROWS, A_ROWS), :]
        return pltpu.make_async_remote_copy(
            src_ref=part, dst_ref=part, send_sem=s_send.at[n], recv_sem=s_recv.at[n],
            device_id=to_sib, device_id_type=MESH,
        )

    def b_copy(s, n, way, device):
        part = b_buf.at[s, pl.ds(n * B_ROWS, B_ROWS), :]
        return pltpu.make_async_remote_copy(
            src_ref=part, dst_ref=part, send_sem=b_send.at[way, s, n], recv_sem=b_recv.at[s, n],
            device_id=device, device_id_type=MESH,
        )

    def f_copy(n, way, device):
        part = f_buf.at[pl.ds(n * F_ROWS, F_ROWS), :]
        return pltpu.make_async_remote_copy(
            src_ref=part, dst_ref=part, send_sem=f_send.at[way, n], recv_sem=f_recv.at[n],
            device_id=device, device_id_type=MESH,
        )

    a_more = (z != 7, z != 1)
    a_next = (to_zp, to_zm)
    y_next = (to_yp, to_ym)

    def b_ways(s, back):
        y_more = y != (1 if back else 3)
        if s == 0:
            return (
                ((y == 0) & (x == 0), to_xp),
                ((y == 0) & ((x == 0) | (x == 3)), to_xm),
                (y_more, y_next[back]),
            )
        return (
            ((y == 0) & ((x == 1) | (x == 2)), to_xp),
            (x == 1, to_xm),
            (y_more & (x >= 1), y_next[back]),
        )

    def pump(m, carry):
        for back in range(2):
            n = 2 * m + back

            @pl.when(z != 0)
            def _():
                a_ring(n, a_next[back]).wait_recv()

            @pl.when(a_more[back])
            def _():
                a_ring(n, a_next[back]).start()

            a_sib(n, c).start()

        @pl.when(m < NBC // 2)
        def _():
            for s in range(2):
                for back in range(2):
                    n = 2 * m + back

                    @pl.when((p != s) & jnp.logical_not(head))
                    def _():
                        b_copy(s, n, 0, to_xp).wait_recv()

                    for way, (sends, device) in enumerate(b_ways(s, back)):
                        @pl.when(sends)
                        def _():
                            b_copy(s, n, way, device).start()

        return carry

    lax.fori_loop(0, NA // 2, pump, 0)

    core0 = c == 0
    f_ways = (
        (core0 & (p == 0) & (z < 4), to_zp),
        (core0 & (p == 0) & ((z == 0) | (z > 5)), to_zm),
        (core0 & (y == 0) & (x < 2), to_xp),
        (core0 & (p == 0), to_xm),
        (core0 & (y < 2), to_yp),
        (core0 & (y == 0), to_ym),
        (core0, to_sib),
    )

    def f_send_all(n):
        for way, (sends, device) in enumerate(f_ways):
            @pl.when(sends)
            def _():
                f_copy(n, way, device).start()

    @pl.when(head)
    def _():
        eye = jnp.where(identity(), 1.0, 0.0)
        work[:, :NB] = a_buf[0, :NB, :]
        work[:, NB:] = eye
        factor_inverse(work)
        f_buf[:NB, :] = work[:, NB:]
        for n in range(2):
            f_send_all(n)
        m_copy(0).wait_recv()
        f_buf[NB : 2 * NB, :] = nt(m_buf[0], f_buf[:NB, :])
        for n in range(2, 4):
            f_send_all(n)
        m_copy(1).wait_recv()
        l10 = f_buf[NB : 2 * NB, :]
        work[:, :NB] = m_buf[1] - nt(l10, l10)
        work[:, NB:] = eye
        factor_inverse(work)
        f_buf[2 * NB :, :] = work[:, NB:]
        for n in range(4, 6):
            f_send_all(n)

        def rest(n, carry):
            b_copy(1, n, 0, to_xp).wait_recv()
            return carry

        lax.fori_loop(0, NBC, rest, 0)

    @pl.when(jnp.logical_not(head))
    def _():
        def relay(n, carry):
            f_copy(n, 0, to_zp).wait_recv()
            f_send_all(n)
            return carry

        lax.fori_loop(0, NF, relay, 0)

    def finish_a(m, carry):
        for back in range(2):
            n = 2 * m + back
            a_sib(n, 1 - c).wait_recv()
            a_sib(n, c).wait_send()

            @pl.when(a_more[back])
            def _():
                a_ring(n, a_next[back]).wait_send()

        return carry

    lax.fori_loop(0, NA // 2, finish_a, 0)

    def finish_b(m, carry):
        for s in range(2):
            for back in range(2):
                n = 2 * m + back
                for way, (sends, device) in enumerate(b_ways(s, back)):
                    @pl.when(sends)
                    def _():
                        b_copy(s, n, way, device).wait_send()

        return carry

    lax.fori_loop(0, NBC // 2, finish_b, 0)

    def finish_f(n, carry):
        for way, (sends, device) in enumerate(f_ways):
            @pl.when(sends)
            def _():
                f_copy(n, way, device).wait_send()

        return carry

    lax.fori_loop(0, NF, finish_f, 0)

    @pl.when((p == 1) & (q == 0))
    def _():
        m_copy(0).wait_send()

    @pl.when((p == 1) & (q == 1))
    def _():
        m_copy(1).wait_send()

    outs = [
        pltpu.make_async_copy(a_buf, a_out, local.at[0]),
        pltpu.make_async_copy(b_buf, b_out, local.at[1]),
        pltpu.make_async_copy(f_buf, f_out, local.at[2]),
    ]
    for out in outs:
        out.start()
    for out in outs:
        out.wait()


def gather(kernel, noise):
    return pl.pallas_call(
        gather_kernel,
        out_shape=(
            jax.ShapeDtypeStruct((2, LOCAL, NB), F32),
            jax.ShapeDtypeStruct((2, NB, LOCAL), F32),
            jax.ShapeDtypeStruct((3 * NB, NB), F32),
        ),
        in_specs=[pl.BlockSpec(memory_space=pl.ANY), pl.BlockSpec(memory_space=pltpu.VMEM)],
        out_specs=[pl.BlockSpec(memory_space=pl.ANY)] * 3,
        scratch_shapes=[
            pltpu.VMEM((2, LOCAL, NB), F32),
            pltpu.VMEM((2, NB, LOCAL), F32),
            pltpu.VMEM((3 * NB, NB), F32),
            pltpu.VMEM((2, NB, NB), F32),
            pltpu.VMEM((NB, 2 * NB), F32),
            pltpu.SemaphoreType.DMA((NA,)),
            pltpu.SemaphoreType.DMA((NA,)),
            pltpu.SemaphoreType.DMA((NA,)),
            pltpu.SemaphoreType.DMA((NA,)),
            pltpu.SemaphoreType.DMA((2, NBC)),
            pltpu.SemaphoreType.DMA((3, 2, NBC)),
            pltpu.SemaphoreType.DMA((NF,)),
            pltpu.SemaphoreType.DMA((7, NF)),
            pltpu.SemaphoreType.DMA((2,)),
            pltpu.SemaphoreType.DMA((2,)),
            pltpu.SemaphoreType.DMA((3,)),
        ],
        compiler_params=pltpu.CompilerParams(
            collective_id=0, has_side_effects=True, vmem_limit_bytes=48 * 2**20
        ),
        name="gather_factor",
    )(kernel, noise)


def update_kernel(m_ref, noise_ref, a_ref, b_ref, f_ref, out_ref, cols):
    p, q = lax.axis_index("row"), lax.axis_index("col")
    t = pl.program_id(0)
    x0, l10, x1 = f_ref[:NB, :], f_ref[NB : 2 * NB, :], f_ref[2 * NB :, :]

    @pl.when(t == 0)
    def _():
        for col in range(T):
            at = slice(col * NB, (col + 1) * NB)
            col0 = nn(x0, b_ref[0, :, at])
            cols[:NB, at] = col0
            cols[NB:, at] = nn(x1, b_ref[1, :, at] - nn(l10, col0))

    row0 = nt(a_ref[0], x0)
    row1 = nt(a_ref[1] - nt(row0, l10), x1)
    rows = jnp.concatenate([row0, row1], axis=1)
    i = t * 16 + p
    i0 = lax.broadcasted_iota(jnp.int32, (NB, NB), 0)
    i1 = lax.broadcasted_iota(jnp.int32, (NB, NB), 1)
    for col in range(T):
        at = slice(col * NB, (col + 1) * NB)
        j = col * 16 + q
        panel = j < 2
        below = jnp.logical_not(panel) & (i >= j)

        @pl.when(below)
        def _():
            on_diag = (i0 == i1) & (i == j)
            block = m_ref[:, at] + jnp.where(on_diag, noise_ref[...], 0.0)
            out_ref[:, at] = block - nn(rows, cols[:, at], HIGH)

        @pl.when(panel & (i >= j))
        def _():
            value = jnp.where(q == 0, row0, row1)
            out_ref[:, at] = jnp.where((i == j) & (i0 < i1), 0.0, value)

        @pl.when(i < j)
        def _():
            out_ref[:, at] = m_ref[:, at]


def update(kernel, noise, a, b, f):
    return pl.pallas_call(
        update_kernel,
        grid=(T,),
        out_shape=jax.ShapeDtypeStruct((LOCAL, LOCAL), F32),
        in_specs=[
            pl.BlockSpec((NB, LOCAL), lambda t: (t, 0)),
            pl.BlockSpec((1, NB), lambda t: (0, t)),
            pl.BlockSpec((2, NB, NB), lambda t: (0, t, 0)),
            pl.BlockSpec((2, NB, LOCAL), lambda t: (0, 0, 0)),
            pl.BlockSpec((3 * NB, NB), lambda t: (0, 0)),
        ],
        out_specs=pl.BlockSpec((NB, LOCAL), lambda t: (t, 0)),
        scratch_shapes=[pltpu.VMEM((2 * NB, LOCAL), F32)],
        compiler_params=pltpu.CompilerParams(vmem_limit_bytes=48 * 2**20),
        name="update",
    )(kernel, noise, a, b, f)


def body(kernel, noise):
    noise = noise.reshape(1, LOCAL)
    a, b, f = gather(kernel, noise)
    return update(kernel, noise, a, b, f)


def solution(mesh):
    return jax.shard_map(
        body,
        mesh=mesh,
        in_specs=(P("row", "col"), P("row")),
        out_specs=P("row", "col"),
        check_vma=False,
    )
```

time: 808 us -> 679 us (0.84)
  the two profiles are of different devices: /device:TPU:141 before, /device:TPU:49 now
where the time goes in v1:
time: 679 us; the launch traced here: 678 us
  Pallas kernels  678 us (100%)
    pallas_call x1, Pallas kernels, gather(): pl.pallas_call(gather_kernel, out_shape=(jax.ShapeDtypeStruct((2, LOCAL,...  657 us
    pallas_call x1, Pallas kernels, update(): pl.pallas_call(update_kernel, grid=(T,), out_shape=jax.ShapeDtypeStruct((...  20.8 us

profile of v1, /device:TPU:49, one launch (start us, length us, event | category | flops | bytes accessed | tf_op | source)
XLA Modules:
  0.0 678.3 jit_solution(2474856196234877738)
XLA Ops:
  0.0 0.7 reshape.3.noise_ref
  0.7 656.8 %gather_factor.1 = (f32[2,1280,256]{2,1,0:T(8,128)S(1)}, f32[2,256,1280]{2,1,0:T(8,128)S(1)}, f32[768,256]{1,0:T(8,128)S(1)}) custom-call(f32[1280,1280]{1,0:T(8,128)} %m_ref.1, f32[1,1280]{1,0:T(1,128)S(1)} %reshape.3.noise_ref), custom_call_target="tpu_custom_call" | custom-call | tf_op jit(solution)/shard_map/gather_factor/pallas_call | solution.py:350
  657.5 20.8 %update.1 = f32[1280,1280]{1,0:T(8,128)} custom-call(f32[1280,1280]{1,0:T(8,128)} %m_ref.1, f32[1,1280]{1,0:T(1,128)S(1)} %reshape.3.noise_ref, f32[2,1280,256]{2,1,0:T(8,128)S(1)} %get-tuple-element.8.a_ref, f32[2,256,1280]{2,1,0:T(8,128)S(1)} %get-tuple-element.9.b_ref, f32[768,256]{1,0:T(8,128)S(1)} %get-tuple-element.10.f_ref), custom_call_target="tpu_custom_call" | custom-call | tf_op jit(solution)/shard_map/update/pallas_call | solution.py:426

commit v2 on v1

--- a/solution.py
+++ b/solution.py
@@ -17,10 +17,11 @@
 
 NA = 20
 A_ROWS = LOCAL // NA
-NBC = 16
+NBC = 32
 B_ROWS = NB // NBC
-NF = 6
-F_ROWS = NB * 3 // NF
+PIECES = ((0, 256), (256, 256), (512, 128), (640, 64), (704, 32), (736, 32))
+NF = len(PIECES)
+SLOTS = 24
 
 
 def dot(a, b, dims, precision=HIGHEST):
@@ -66,7 +67,7 @@
     return jnp.concatenate(done, axis=0)
 
 
-def factor_inverse(work):
+def factor_inverse(work, done=lambda k: None):
     following = None
     for k in range(8):
         r0 = 32 * k
@@ -74,6 +75,7 @@
         rows = work[r0 : r0 + 32, lo:hi] if following is None else following
         rows = eliminate(rows, r0 - lo)
         work[r0 : r0 + 32, lo:hi] = rows
+        done(k)
         if k == 7:
             break
         r1 = r0 + 32
@@ -122,12 +124,39 @@
         b_load.start()
 
     barrier = pltpu.get_barrier_semaphore()
+
+    def greet(device):
+        pl.semaphore_signal(barrier, inc=1, device_id=device, device_id_type=MESH)
+
     for device in (to_xp, to_xm, to_yp, to_ym, to_zp, to_zm, to_sib):
-        pl.semaphore_signal(barrier, inc=1, device_id=device, device_id_type=MESH)
+        greet(device)
+
+    core0 = c == 0
+    top = core0 & (p == 0)
+    edge = core0 & (y == 0)
 
     @pl.when(head)
     def _():
-        pl.semaphore_signal(barrier, inc=1, device_id=(1, 1), device_id_type=MESH)
+        for k in range(2, 7):
+            greet((0, 2 * k))
+        greet((1, 1))
+
+    @pl.when(((p == 1) & (q == 1)) | (top & (z >= 2) & (z <= 6)))
+    def _():
+        greet((0, 0))
+
+    @pl.when(edge & ((x == 0) | (x == 2)))
+    def _():
+        greet((2 - x, q))
+
+    @pl.when(core0 & ((y == 0) | (y == 2)))
+    def _():
+        greet((4 * (2 - y) + x, q))
+
+    peers = 7 + jnp.where(head, 6, 0)
+    peers += jnp.where(((p == 1) & (q == 1)) | (top & (z >= 2) & (z <= 6)), 1, 0)
+    peers += jnp.where(edge & ((x == 0) | (x == 2)), 1, 0)
+    peers += jnp.where(core0 & ((y == 0) | (y == 2)), 1, 0)
 
     @pl.when(z == 0)
     def _():
@@ -141,7 +170,7 @@
     def _():
         a_buf[c, :NB, :] = a_buf[c, :NB, :] + jnp.where(identity(), noise_ref[:, :NB], 0.0)
 
-    pl.semaphore_wait(barrier, jnp.where((p == 1) & (q == 1), 8, 7))
+    pl.semaphore_wait(barrier, peers)
 
     def m_copy(which):
         return pltpu.make_async_remote_copy(
@@ -179,7 +208,7 @@
         )
 
     def f_copy(n, way, device):
-        part = f_buf.at[pl.ds(n * F_ROWS, F_ROWS), :]
+        part = f_buf.at[pl.ds(*PIECES[n]), :]
         return pltpu.make_async_remote_copy(
             src_ref=part, dst_ref=part, send_sem=f_send.at[way, n], recv_sem=f_recv.at[n],
             device_id=device, device_id_type=MESH,
@@ -187,65 +216,72 @@
 
     a_more = (z != 7, z != 1)
     a_next = (to_zp, to_zm)
-    y_next = (to_yp, to_ym)
-
-    def b_ways(s, back):
-        y_more = y != (1 if back else 3)
-        if s == 0:
-            return (
-                ((y == 0) & (x == 0), to_xp),
-                ((y == 0) & ((x == 0) | (x == 3)), to_xm),
-                (y_more, y_next[back]),
-            )
-        return (
-            ((y == 0) & ((x == 1) | (x == 2)), to_xp),
-            (x == 1, to_xm),
-            (y_more & (x >= 1), y_next[back]),
+    a_hops = (z, (8 - z) % 8)
+    plane = (to_xp, to_yp, to_xm, to_ym)
+
+    def tree(s, k):
+        dx, dy = (x + 4 - s) % 4, y
+        u, v = ((dx, dy), (dy, (4 - dx) % 4), ((4 - dx) % 4, (4 - dy) % 4), ((4 - dy) % 4, dx))[k]
+        side = jnp.minimum(v, 4 - v)
+        hops = jnp.where((u == 0) & (v == 0), 0, jnp.where(u == 0, 2, u) + side)
+        sends = (
+            (u == 2) | ((u == 1) & (v < 3)) | ((u == 0) & (v == 0)),
+            (u == 1) & (v < 2),
+            (u == 1) & (v >= 1),
+            (v == 0) & ((u == 1) | (u == 2)),
         )
-
-    def pump(m, carry):
+        return hops, [sends[(d - k) % 4] for d in range(4)]
+
+    def b_tree(s, k):
+        hops, sends = tree(s, k)
+        if (s, k) == (1, 2):
+            hops0, sends0 = tree(1, 0)
+            hops = jnp.where(q == 0, hops0, hops)
+            sends = [((q == 0) & a) | ((q != 0) & b) for a, b in zip(sends0, sends)]
+        return hops, sends
+
+    trees = {(s, k): b_tree(s, k) for s in range(2) for k in range(4)}
+
+    def pump(slot, carry):
         for back in range(2):
+            m = slot - 2 * a_hops[back]
             n = 2 * m + back
 
-            @pl.when(z != 0)
+            @pl.when((m >= 0) & (m < NA // 2))
             def _():
-                a_ring(n, a_next[back]).wait_recv()
-
-            @pl.when(a_more[back])
+                @pl.when(z != 0)
+                def _():
+                    a_ring(n, a_next[back]).wait_recv()
+
+                @pl.when(a_more[back])
+                def _():
+                    a_ring(n, a_next[back]).start()
+
+                a_sib(n, c).start()
+
+        for (s, k), (hops, sends) in trees.items():
+            m = slot - 2 * hops
+            n = 4 * m + k
+
+            @pl.when((m >= 0) & (m < NBC // 4))
             def _():
-                a_ring(n, a_next[back]).start()
-
-            a_sib(n, c).start()
-
-        @pl.when(m < NBC // 2)
-        def _():
-            for s in range(2):
-                for back in range(2):
-                    n = 2 * m + back
-
-                    @pl.when((p != s) & jnp.logical_not(head))
+                @pl.when((p != s) & jnp.logical_not(head))
+                def _():
+                    b_copy(s, n, 0, to_xp).wait_recv()
+
+                for way in range(4):
+                    @pl.when(sends[way])
                     def _():
-                        b_copy(s, n, 0, to_xp).wait_recv()
-
-                    for way, (sends, device) in enumerate(b_ways(s, back)):
-                        @pl.when(sends)
-                        def _():
-                            b_copy(s, n, way, device).start()
+                        b_copy(s, n, way, plane[way]).start()
 
         return carry
 
-    lax.fori_loop(0, NA // 2, pump, 0)
-
-    core0 = c == 0
-    f_ways = (
-        (core0 & (p == 0) & (z < 4), to_zp),
-        (core0 & (p == 0) & ((z == 0) | (z > 5)), to_zm),
-        (core0 & (y == 0) & (x < 2), to_xp),
-        (core0 & (p == 0), to_xm),
-        (core0 & (y < 2), to_yp),
-        (core0 & (y == 0), to_ym),
-        (core0, to_sib),
-    )
+    lax.fori_loop(0, SLOTS, pump, 0)
+
+    f_ways = [(head, (0, 2 * k)) for k in (4, 3, 5, 2, 6, 1, 7)]
+    f_ways += [(top, (k, q)) for k in (2, 1, 3)]
+    f_ways += [(edge, (4 * k + x, q)) for k in (2, 1, 3)]
+    f_ways += [(core0, to_sib)]
 
     def f_send_all(n):
         for way, (sends, device) in enumerate(f_ways):
@@ -260,20 +296,24 @@
         work[:, NB:] = eye
         factor_inverse(work)
         f_buf[:NB, :] = work[:, NB:]
-        for n in range(2):
-            f_send_all(n)
+        f_send_all(0)
         m_copy(0).wait_recv()
-        f_buf[NB : 2 * NB, :] = nt(m_buf[0], f_buf[:NB, :])
-        for n in range(2, 4):
-            f_send_all(n)
+        l10 = nt(m_buf[0], work[:, NB:])
+        f_buf[NB : 2 * NB, :] = l10
+        f_send_all(1)
         m_copy(1).wait_recv()
-        l10 = f_buf[NB : 2 * NB, :]
         work[:, :NB] = m_buf[1] - nt(l10, l10)
         work[:, NB:] = eye
-        factor_inverse(work)
-        f_buf[2 * NB :, :] = work[:, NB:]
-        for n in range(4, 6):
-            f_send_all(n)
+
+        def strip(k):
+            last = 32 * (k + 1)
+            for n in range(2, NF):
+                start, size = PIECES[n]
+                if start - 2 * NB + size == last:
+                    f_buf[start : start + size, :] = work[last - size : last, NB:]
+                    f_send_all(n)
+
+        factor_inverse(work, strip)
 
         def rest(n, carry):
             b_copy(1, n, 0, to_xp).wait_recv()
@@ -283,12 +323,9 @@
 
     @pl.when(jnp.logical_not(head))
     def _():
-        def relay(n, carry):
+        for n in range(NF):
             f_copy(n, 0, to_zp).wait_recv()
             f_send_all(n)
-            return carry
-
-        lax.fori_loop(0, NF, relay, 0)
 
     def finish_a(m, carry):
         for back in range(2):
@@ -305,27 +342,21 @@
     lax.fori_loop(0, NA // 2, finish_a, 0)
 
     def finish_b(m, carry):
-        for s in range(2):
-            for back in range(2):
-                n = 2 * m + back
-                for way, (sends, device) in enumerate(b_ways(s, back)):
-                    @pl.when(sends)
-                    def _():
-                        b_copy(s, n, way, device).wait_send()
+        for (s, k), (hops, sends) in trees.items():
+            for way in range(4):
+                @pl.when(sends[way])
+                def _():
+                    b_copy(s, 4 * m + k, way, plane[way]).wait_send()
 
         return carry
 
-    lax.fori_loop(0, NBC // 2, finish_b, 0)
-
-    def finish_f(n, carry):
+    lax.fori_loop(0, NBC // 4, finish_b, 0)
+
+    for n in range(NF):
         for way, (sends, device) in enumerate(f_ways):
             @pl.when(sends)
             def _():
                 f_copy(n, way, device).wait_send()
-
-        return carry
-
-    lax.fori_loop(0, NF, finish_f, 0)
 
     @pl.when((p == 1) & (q == 0))
     def _():
@@ -367,9 +398,9 @@
             pltpu.SemaphoreType.DMA((NA,)),
             pltpu.SemaphoreType.DMA((NA,)),
             pltpu.SemaphoreType.DMA((2, NBC)),
-            pltpu.SemaphoreType.DMA((3, 2, NBC)),
+            pltpu.SemaphoreType.DMA((4, 2, NBC)),
             pltpu.SemaphoreType.DMA((NF,)),
-            pltpu.SemaphoreType.DMA((7, NF)),
+            pltpu.SemaphoreType.DMA((14, NF)),
             pltpu.SemaphoreType.DMA((2,)),
             pltpu.SemaphoreType.DMA((2,)),
             pltpu.SemaphoreType.DMA((3,)),
@@ -381,22 +412,47 @@
     )(kernel, noise)
 
 
-def update_kernel(m_ref, noise_ref, a_ref, b_ref, f_ref, out_ref, cols):
+def split(value):
+    high = value.astype(jnp.bfloat16)
+    return high, (value - high.astype(F32)).astype(jnp.bfloat16)
+
+
+def three(a, b, dims):
+    def one(u, v):
+        return lax.dot_general(u, v, (dims, ((), ())), preferred_element_type=F32)
+
+    return one(a[0], b[0]) + (one(a[0], b[1]) + one(a[1], b[0]))
+
+
+NN = ((1,), (0,))
+NT = ((1,), (1,))
+
+
+def update_kernel(m_ref, noise_ref, a_ref, b_ref, f_ref, out_ref, cols_high, cols_low, f_high, f_low):
     p, q = lax.axis_index("row"), lax.axis_index("col")
     t = pl.program_id(0)
-    x0, l10, x1 = f_ref[:NB, :], f_ref[NB : 2 * NB, :], f_ref[2 * NB :, :]
+
+    @pl.when(t == 0)
+    def _():
+        f_high[...], f_low[...] = split(f_ref[...])
+
+    x0, l10, x1 = [(f_high[k * NB : (k + 1) * NB, :], f_low[k * NB : (k + 1) * NB, :]) for k in range(3)]
 
     @pl.when(t == 0)
     def _():
         for col in range(T):
             at = slice(col * NB, (col + 1) * NB)
-            col0 = nn(x0, b_ref[0, :, at])
-            cols[:NB, at] = col0
-            cols[NB:, at] = nn(x1, b_ref[1, :, at] - nn(l10, col0))
-
-    row0 = nt(a_ref[0], x0)
-    row1 = nt(a_ref[1] - nt(row0, l10), x1)
-    rows = jnp.concatenate([row0, row1], axis=1)
+            col0 = split(three(x0, split(b_ref[0, :, at]), NN))
+            col1 = split(three(x1, split(b_ref[1, :, at] - three(l10, col0, NN)), NN))
+            for half, value in enumerate((col0, col1)):
+                cols_high[half * NB : (half + 1) * NB, at] = value[0]
+                cols_low[half * NB : (half + 1) * NB, at] = value[1]
+
+    row0 = three(split(a_ref[0]), x0, NT)
+    row0_parts = split(row0)
+    row1 = three(split(a_ref[1] - three(row0_parts, l10, NT)), x1, NT)
+    row1_parts = split(row1)
+    rows = [jnp.concatenate([u, v], axis=1) for u, v in zip(row0_parts, row1_parts)]
     i = t * 16 + p
     i0 = lax.broadcasted_iota(jnp.int32, (NB, NB), 0)
     i1 = lax.broadcasted_iota(jnp.int32, (NB, NB), 1)
@@ -410,7 +466,7 @@
         def _():
             on_diag = (i0 == i1) & (i == j)
             block = m_ref[:, at] + jnp.where(on_diag, noise_ref[...], 0.0)
-            out_ref[:, at] = block - nn(rows, cols[:, at], HIGH)
+            out_ref[:, at] = block - three(rows, (cols_high[:, at], cols_low[:, at]), NN)
 
         @pl.when(panel & (i >= j))
         def _():
@@ -435,7 +491,12 @@
             pl.BlockSpec((3 * NB, NB), lambda t: (0, 0)),
         ],
         out_specs=pl.BlockSpec((NB, LOCAL), lambda t: (t, 0)),
-        scratch_shapes=[pltpu.VMEM((2 * NB, LOCAL), F32)],
+        scratch_shapes=[
+            pltpu.VMEM((2 * NB, LOCAL), jnp.bfloat16),
+            pltpu.VMEM((2 * NB, LOCAL), jnp.bfloat16),
+            pltpu.VMEM((3 * NB, NB), jnp.bfloat16),
+            pltpu.VMEM((3 * NB, NB), jnp.bfloat16),
+        ],
         compiler_params=pltpu.CompilerParams(vmem_limit_bytes=48 * 2**20),
         name="update",
     )(kernel, noise, a, b, f)

time: 679 us -> 112 us (0.16)
  the two profiles are of different devices: /device:TPU:49 before, /device:TPU:43 now
where the time goes in v2:
time: 112 us
  Pallas kernels  111 us (99%)
    pallas_call x1, Pallas kernels, gather(): pl.pallas_call(gather_kernel, out_shape=(jax.ShapeDtypeStruct((2, LOCAL,...  94.9 us
    pallas_call x1, Pallas kernels, update(): pl.pallas_call(update_kernel, grid=(T,), out_shape=jax.ShapeDtypeStruct((...  16 us

profile of v2, /device:TPU:43, one launch (start us, length us, event | category | flops | bytes accessed | tf_op | source)
XLA Modules:
  0.0 111.6 jit_solution(11019067713693248848)
XLA Ops:
  0.0 0.7 reshape.3.noise_ref
  0.7 94.9 %gather_factor.1 = (f32[2,1280,256]{2,1,0:T(8,128)S(1)}, f32[2,256,1280]{2,1,0:T(8,128)S(1)}, f32[768,256]{1,0:T(8,128)S(1)}) custom-call(f32[1280,1280]{1,0:T(8,128)} %m_ref.1, f32[1,1280]{1,0:T(1,128)S(1)} %reshape.3.noise_ref), custom_call_target="tpu_custom_call" | custom-call | tf_op jit(solution)/shard_map/gather_factor/pallas_call | solution.py:381
  95.6 16.0 %update.1 = f32[1280,1280]{1,0:T(8,128)} custom-call(f32[1280,1280]{1,0:T(8,128)} %m_ref.1, f32[1,1280]{1,0:T(1,128)S(1)} %reshape.3.noise_ref, f32[2,1280,256]{2,1,0:T(8,128)S(1)} %get-tuple-element.8.a_ref, f32[2,256,1280]{2,1,0:T(8,128)S(1)} %get-tuple-element.9.b_ref, f32[768,256]{1,0:T(8,128)S(1)} %get-tuple-element.10.f_ref), custom_call_target="tpu_custom_call" | custom-call | tf_op jit(solution)/shard_map/update/pallas_call | solution.py:482

commit v3 on v2

v3 whole, which is shorter than its diff:
```python
import functools

import jax
import jax.numpy as jnp
from jax import lax
from jax.experimental import pallas as pl
from jax.experimental.pallas import tpu as pltpu
from jax.sharding import PartitionSpec as P

NB = 256
T = 5
LOCAL = NB * T
MESH = pl.DeviceIdType.MESH
HIGHEST = lax.Precision.HIGHEST
HIGH = lax.Precision.HIGH
F32 = jnp.float32

NA = 20
A_ROWS = LOCAL // NA
A_SLOTS = 24
NBC = 16
B_ROWS = NB // NBC
B_SLOTS = 9
PIECES = tuple((64 * n, 64) for n in range(11)) + ((704, 32), (736, 32))
NF = len(PIECES)


def dot(a, b, dims, precision=HIGHEST):
    return lax.dot_general(a, b, (dims, ((), ())), precision=precision, preferred_element_type=F32)


def nn(a, b, precision=HIGHEST):
    return dot(a, b, ((1,), (0,)), precision)


def nt(a, b, precision=HIGHEST):
    return dot(a, b, ((1,), (1,)), precision)


def tn(a, b, precision=HIGHEST):
    return dot(a, b, ((0,), (0,)), precision)


def eliminate(rows, first):
    width = rows.shape[1]
    done = []
    for g in range(4):
        n = rows.shape[0]
        sub = lax.broadcasted_iota(jnp.int32, (n, 128), 0)
        at = first + 8 * g
        cols = [jnp.broadcast_to(rows[:, at + c : at + c + 1], (n, 128)) for c in range(8)]
        for j in range(8):
            inv = pltpu.reciprocal(cols[j][j : j + 1, :], approx=True)
            scale = jnp.where(sub > j, cols[j] * inv, 0.0)
            for c in range(j + 1, 8):
                cols[c] = cols[c] - scale * cols[c][j : j + 1, :]
            pivot = rows[j : j + 1, :]
            rows = jnp.concatenate(
                [rows[:, w : w + 128] - scale * pivot[:, w : w + 128] for w in range(0, width, 128)], axis=1
            )
        sub8 = lax.broadcasted_iota(jnp.int32, (8, 128), 0)
        diag = cols[0][:8]
        for j in range(1, 8):
            diag = jnp.where(sub8 == j, cols[j][:8], diag)
        root = lax.rsqrt(diag)
        done.append(rows[:8] * jnp.concatenate([root] * (width // 128), axis=1))
        rows = rows[8:]
    return jnp.concatenate(done, axis=0)


def factor_inverse(work, done=lambda k: None):
    following = None
    for k in range(8):
        r0 = 32 * k
        lo, hi = r0 // 128 * 128, NB + (r0 + 32 + 127) // 128 * 128
        rows = work[r0 : r0 + 32, lo:hi] if following is None else following
        rows = eliminate(rows, r0 - lo)
        work[r0 : r0 + 32, lo:hi] = rows
        done(k)
        if k == 7:
            break
        r1 = r0 + 32
        lo1, hi1 = r1 // 128 * 128, NB + (r1 + 32 + 127) // 128 * 128
        product = tn(rows[:, r1 - lo : r1 - lo + 32], rows)
        if hi1 > hi:
            product = jnp.concatenate([product, jnp.zeros((32, hi1 - hi), F32)], axis=1)
        following = work[r1 : r1 + 32, lo1:hi1] - product[:, lo1 - lo :]
        if k < 6:
            r2 = r1 + 32
            lo2 = r2 // 128 * 128
            product = tn(rows[:, lo2 - lo : NB - lo], rows[:, lo2 - lo :])
            work[r2:NB, lo2:hi] = work[r2:NB, lo2:hi] - product[r2 - lo2 :, :]


def identity():
    i0 = lax.broadcasted_iota(jnp.int32, (NB, NB), 0)
    i1 = lax.broadcasted_iota(jnp.int32, (NB, NB), 1)
    return i0 == i1


def gather_kernel(
    kernel_ref, noise_ref, a_out, b_out, f_out,
    a_buf, b_buf, f_buf, m_buf, work,
    a_recv, a_send, s_recv, s_send, b_recv, b_send, f_recv, f_send, m_recv, m_send, local,
):
    p, q = lax.axis_index("row"), lax.axis_index("col")
    y, x, z, c = p // 4, p % 4, q // 2, q % 2
    rows_next = (y * 4 + (x + 1) % 4, (y + 1) % 4 * 4 + x, y * 4 + (x + 3) % 4, (y + 3) % 4 * 4 + x)
    z_next = ((z + 1) % 8, (z + 7) % 8)
    sib = (p, z * 2 + 1 - c)
    core0, core1 = c == 0, c == 1
    head = (p == 0) & (q == 0)
    a_source, b_source = z == 0, p < 2

    def a_load(s):
        return pltpu.make_async_copy(kernel_ref.at[:, pl.ds(0, NB)], a_buf.at[s], local.at[0])

    def b_load(g, s):
        return pltpu.make_async_copy(kernel_ref.at[pl.ds(0, NB), :], b_buf.at[2 * g + s], local.at[1])

    def each_source(run_a, run_b):
        for s in range(2):
            @pl.when(a_source & (c == s))
            def _():
                run_a(s)

            for g in range(2):
                @pl.when((p == s) & (c == g))
                def _():
                    run_b(g, s)


    each_source(lambda s: a_load(s).start(), lambda g, s: b_load(g, s).start())

    barrier = pltpu.get_barrier_semaphore()
    peers = jnp.int32(7)

    def greet(device):
        pl.semaphore_signal(barrier, inc=1, device_id=device, device_id_type=MESH)

    for row in rows_next:
        greet((row, q))
    for level in z_next:
        greet((p, level * 2 + c))
    greet(sib)

    def greet_if(condition, devices):
        @pl.when(condition)
        def _():
            for device in devices:
                greet(device)

        return jnp.where(condition, len(devices), 0)

    peers += greet_if(a_source & core1, [(p, 2), (p, 14)])
    peers += greet_if(core0 & ((z == 1) | (z == 7)), [(p, 1)])
    peers += greet_if(b_source & core0, [(row, z * 2 + 1) for row in rows_next])
    for s in range(2):
        beside = ((y == 0) & ((x + 4 - s) % 2 == 1)) | ((x == s) & (y % 2 == 1))
        peers += greet_if(core1 & beside, [(s, z * 2)])
    peers += greet_if(head, [(0, 5), (0, 13)])
    peers += greet_if((p == 0) & ((q == 5) | (q == 13)), [(0, 0)])
    peers += greet_if((p == 0) & (q == 5), [(0, 9)])
    peers += greet_if((p == 0) & (q == 9), [(0, 5)])
    peers += greet_if(core1 & (y == 0) & (x % 2 == 0), [((x + 2) % 4, q)])
    peers += greet_if(core1 & (y % 2 == 0), [((y + 2) % 4 * 4 + x, q)])

    each_source(lambda s: a_load(s).wait(), lambda g, s: b_load(g, s).wait())
    for s in range(2):
        @pl.when((p == s) & (q == s))
        def _():
            a_buf[s, :NB, :] = a_buf[s, :NB, :] + jnp.where(identity(), noise_ref[:, :NB], 0.0)

    pl.semaphore_wait(barrier, peers)

    def remote(src, dst, send_sem, recv_sem, device):
        return pltpu.make_async_remote_copy(
            src_ref=src, dst_ref=dst, send_sem=send_sem, recv_sem=recv_sem, device_id=device, device_id_type=MESH
        )

    def m_copy(which):
        return remote(a_buf.at[which, pl.ds(0, NB), :], m_buf.at[which], m_send.at[which], m_recv.at[which], (0, 0))

    for which in range(2):
        @pl.when((p == 1) & (q == which))
        def _():
            m_copy(which).start()

    def a_ring(s, n, back):
        part = a_buf.at[s, pl.ds(n * A_ROWS, A_ROWS), :]
        return remote(part, part, a_send.at[s, n], a_recv.at[s, n], (p, z_next[back] * 2))

    def a_sib(s, n):
        part = a_buf.at[s, pl.ds(n * A_ROWS, A_ROWS), :]
        return remote(part, part, s_send.at[s, n], s_recv.at[s, n], sib)

    def b_plane(g, s, n, way):
        part = b_buf.at[2 * g + s, pl.ds(n * B_ROWS, B_ROWS), :]
        return remote(part, part, b_send.at[way, 2 * g + s, n], b_recv.at[2 * g + s, n], (rows_next[way], z * 2 + 1))

    def b_sib(s, n):
        part = b_buf.at[s, pl.ds(n * B_ROWS, B_ROWS), :]
        return remote(part, part, b_send.at[4, s, n], b_recv.at[s, n], sib)

    a_more = (z != 7, z != 1)
    a_hops = (z, 8 - z)

    def tree(s, k):
        dx, dy = (x + 4 - s) % 4, y
        u, v = ((dx, dy), (dy, (4 - dx) % 4), ((4 - dx) % 4, (4 - dy) % 4), ((4 - dy) % 4, dx))[k]
        hops = jnp.where(u == 0, 2, u) + jnp.minimum(v, 4 - v)
        sends = (
            (u == 2) | ((u == 1) & (v < 3)),
            (u == 1) & (v < 2),
            (u == 1) & (v >= 1),
            (v == 0) & ((u == 1) | (u == 2)),
        )
        return hops, [sends[(d - k) % 4] for d in range(4)]

    trees = {(s, k): tree(s, k) for s in range(2) for k in range(4)}

    def source(m, carry):
        def a_start(s):
            for n in range(4):
                a_ring(s, 4 * m + n, n % 2).start()
                a_sib(s, 4 * m + n).start()

        def b_start(g, s):
            for k in range(4):
                b_plane(g, s, 4 * m + k, k).start()

        each_source(a_start, b_start)
        return carry

    lax.fori_loop(0, NBC // 4, source, 0)
    for s in range(2):
        @pl.when(a_source & (c == s))
        def _():
            for n in range(NBC, NA):
                a_ring(s, n, n % 2).start()
                a_sib(s, n).start()

    def pass_a(slot, carry):
        @pl.when(core0 & (z != 0))
        def _():
            for back in range(2):
                m = slot - 2 * a_hops[back]
                n = 2 * ((m + NA) % (NA // 2)) + back

                @pl.when((m >= 0) & (m < NA // 2))
                def _():
                    for s in range(2):
                        a_ring(s, n, back).wait_recv()

                        @pl.when(a_more[back])
                        def _():
                            a_ring(s, n, back).start()

                        a_sib(s, n).start()

        return carry

    def pass_b(slot, carry):
        @pl.when(core1)
        def _():
            for (s, k), (hops, sends) in trees.items():
                m = slot - hops
                n = 4 * ((m + NBC) % (NBC // 4)) + k

                @pl.when((p != s) & (m >= 0) & (m < NBC // 4))
                def _():
                    for g in range(2):
                        b_plane(g, s, n, 0).wait_recv()
                        for way in range(4):
                            @pl.when(sends[way])
                            def _():
                                b_plane(g, s, n, way).start()

                    b_sib(s, n).start()

        return carry

    lax.fori_loop(0, A_SLOTS, pass_a, 0)
    lax.fori_loop(0, B_SLOTS, pass_b, 0)

    def a_wait_sib(s):
        def wait(n, carry):
            a_sib(s, n).wait_recv()
            return carry

        lax.fori_loop(0, NA, wait, 0)

    def b_wait_sib(n, carry):
        for s in range(2):
            @pl.when(p != s)
            def _():
                b_sib(s, n).wait_recv()

        return carry

    top = core1 & (p == 0)
    edge = core1 & (y == 0)
    f_ways = [(head, (0, 5)), (head, (0, 13)), (head, (0, 1))]
    f_ways += [(top & (z == 2), (0, k)) for k in (9, 7, 3)] + [(top & (z == 6), (0, k)) for k in (11, 15)]
    f_ways += [(top, (k, q)) for k in (2, 1, 3)]
    f_ways += [(edge, (4 * k + x, q)) for k in (2, 1, 3)]
    f_ways += [(core1 & ((p != 0) | (q != 1)), sib)]
    F_HEAD = 3

    def f_copy(n, way, device):
        part = f_buf.at[pl.ds(*PIECES[n]), :]
        return remote(part, part, f_send.at[way, n], f_recv.at[n], device)

    a_store = pltpu.make_async_copy(a_buf, a_out, local.at[0])

    def b_store(g):
        return pltpu.make_async_copy(b_buf.at[pl.ds(2 * g, 2)], b_out, local.at[1])

    f_store = pltpu.make_async_copy(f_buf, f_out, local.at[2])

    @pl.when(head)
    def _():
        eye = jnp.where(identity(), 1.0, 0.0)

        def put(first, last, value):
            f_buf[first:last, :] = value
            for n in range(NF):
                if first <= PIECES[n][0] < last:
                    for way in range(F_HEAD):
                        f_copy(n, way, f_ways[way][1]).start()

        work[:, :NB] = a_buf[0, :NB, :]
        work[:, NB:] = eye
        factor_inverse(work)
        put(0, NB, work[:, NB:])
        m_copy(0).wait_recv()
        l10 = nt(m_buf[0], work[:, NB:])
        put(NB, 2 * NB, l10)
        m_copy(1).wait_recv()
        work[:, :NB] = m_buf[1] - nt(l10, l10)
        work[:, NB:] = eye

        def strip(k):
            last = 32 * (k + 1)
            for start, size in PIECES:
                if start - 2 * NB + size == last:
                    put(start, start + size, work[last - size : last, NB:])

        factor_inverse(work, strip)
        a_wait_sib(1)
        lax.fori_loop(0, NBC, b_wait_sib, 0)
        a_store.start()
        b_store(0).start()

    @pl.when(core0 & jnp.logical_not(head))
    def _():
        @pl.when(z == 0)
        def _():
            a_wait_sib(1)

        a_store.start()
        lax.fori_loop(0, NBC, b_wait_sib, 0)
        b_store(0).start()
        for n in range(NF):
            f_copy(n, 0, sib).wait_recv()

    @pl.when(core1)
    def _():
        b_store(1).start()
        for n in range(NF):
            f_copy(n, 0, sib).wait_recv()
            for way in range(F_HEAD, len(f_ways)):
                @pl.when(f_ways[way][0])
                def _():
                    f_copy(n, way, f_ways[way][1]).start()

        a_wait_sib(0)

        @pl.when(z != 0)
        def _():
            a_wait_sib(1)

        a_store.start()

    f_store.start()

    def finish_a(m, carry):
        for back in range(2):
            n = 2 * m + back
            for s in range(2):
                @pl.when((a_source & (c == s)) | (core0 & (z != 0)))
                def _():
                    a_sib(s, n).wait_send()

                    @pl.when(a_more[back])
                    def _():
                        a_ring(s, n, back).wait_send()

        return carry

    lax.fori_loop(0, NA // 2, finish_a, 0)

    def finish_b(m, carry):
        for s in range(2):
            for g in range(2):
                @pl.when((p == s) & (c == g))
                def _():
                    for k in range(4):
                        b_plane(g, s, 4 * m + k, k).wait_send()

        @pl.when(core1)
        def _():
            for (s, k), (hops, sends) in trees.items():
                @pl.when(p != s)
                def _():
                    for g in range(2):
                        for way in range(4):
                            @pl.when(sends[way])
                            def _():
                                b_plane(g, s, 4 * m + k, way).wait_send()

                    b_sib(s, 4 * m + k).wait_send()

        return carry

    lax.fori_loop(0, NBC // 4, finish_b, 0)

    for n in range(NF):
        for way, (sends, device) in enumerate(f_ways):
            @pl.when(sends)
            def _():
                f_copy(n, way, device).wait_send()

    for which in range(2):
        @pl.when((p == 1) & (q == which))
        def _():
            m_copy(which).wait_send()

    a_store.wait()
    for g in range(2):
        @pl.when(c == g)
        def _():
            b_store(g).wait()

    f_store.wait()


def gather(kernel, noise):
    return pl.pallas_call(
        gather_kernel,
        out_shape=(
            jax.ShapeDtypeStruct((2, LOCAL, NB), F32),
            jax.ShapeDtypeStruct((2, NB, LOCAL), F32),
            jax.ShapeDtypeStruct((3 * NB, NB), F32),
        ),
        in_specs=[pl.BlockSpec(memory_space=pl.ANY), pl.BlockSpec(memory_space=pltpu.VMEM)],
        out_specs=[pl.BlockSpec(memory_space=pl.ANY)] * 3,
        scratch_shapes=[
            pltpu.VMEM((2, LOCAL, NB), F32),
            pltpu.VMEM((4, NB, LOCAL), F32),
            pltpu.VMEM((3 * NB, NB), F32),
            pltpu.VMEM((2, NB, NB), F32),
            pltpu.VMEM((NB, 2 * NB), F32),
            pltpu.SemaphoreType.DMA((2, NA)),
            pltpu.SemaphoreType.DMA((2, NA)),
            pltpu.SemaphoreType.DMA((2, NA)),
            pltpu.SemaphoreType.DMA((2, NA)),
            pltpu.SemaphoreType.DMA((4, NBC)),
            pltpu.SemaphoreType.DMA((5, 4, NBC)),
            pltpu.SemaphoreType.DMA((NF,)),
            pltpu.SemaphoreType.DMA((15, NF)),
            pltpu.SemaphoreType.DMA((2,)),
            pltpu.SemaphoreType.DMA((2,)),
            pltpu.SemaphoreType.DMA((3,)),
        ],
        compiler_params=pltpu.CompilerParams(
            collective_id=0, has_side_effects=True, vmem_limit_bytes=48 * 2**20
        ),
        name="gather_factor",
    )(kernel, noise)


def split(value):
    high = value.astype(jnp.bfloat16)
    return high, (value - high.astype(F32)).astype(jnp.bfloat16)


def three(a, b, dims):
    def one(u, v):
        return lax.dot_general(u, v, (dims, ((), ())), preferred_element_type=F32)

    return one(a[0], b[0]) + (one(a[0], b[1]) + one(a[1], b[0]))


NN = ((1,), (0,))
NT = ((1,), (1,))


def update_kernel(m_ref, noise_ref, a_ref, b_ref, f_ref, out_ref, cols_high, cols_low, f_high, f_low):
    p, q = lax.axis_index("row"), lax.axis_index("col")
    t = pl.program_id(0)

    @pl.when(t == 0)
    def _():
        f_high[...], f_low[...] = split(f_ref[...])

    x0, l10, x1 = [(f_high[k * NB : (k + 1) * NB, :], f_low[k * NB : (k + 1) * NB, :]) for k in range(3)]

    @pl.when(t == 0)
    def _():
        for col in range(T):
            at = slice(col * NB, (col + 1) * NB)
            col0 = split(three(x0, split(b_ref[0, :, at]), NN))
            col1 = split(three(x1, split(b_ref[1, :, at] - three(l10, col0, NN)), NN))
            for half, value in enumerate((col0, col1)):
                cols_high[half * NB : (half + 1) * NB, at] = value[0]
                cols_low[half * NB : (half + 1) * NB, at] = value[1]

    row0 = three(split(a_ref[0]), x0, NT)
    row0_parts = split(row0)
    row1 = three(split(a_ref[1] - three(row0_parts, l10, NT)), x1, NT)
    row1_parts = split(row1)
    rows = [jnp.concatenate([u, v], axis=1) for u, v in zip(row0_parts, row1_parts)]
    i = t * 16 + p
    i0 = lax.broadcasted_iota(jnp.int32, (NB, NB), 0)
    i1 = lax.broadcasted_iota(jnp.int32, (NB, NB), 1)
    for col in range(T):
        at = slice(col * NB, (col + 1) * NB)
        j = col * 16 + q
        panel = j < 2
        below = jnp.logical_not(panel) & (i >= j)

        @pl.when(below)
        def _():
            on_diag = (i0 == i1) & (i == j)
            block = m_ref[:, at] + jnp.where(on_diag, noise_ref[...], 0.0)
            out_ref[:, at] = block - three(rows, (cols_high[:, at], cols_low[:, at]), NN)

        @pl.when(panel & (i >= j))
        def _():
            value = jnp.where(q == 0, row0, row1)
            out_ref[:, at] = jnp.where((i == j) & (i0 < i1), 0.0, value)

        @pl.when(i < j)
        def _():
            out_ref[:, at] = m_ref[:, at]


def update(kernel, noise, a, b, f):
    return pl.pallas_call(
        update_kernel,
        grid=(T,),
        out_shape=jax.ShapeDtypeStruct((LOCAL, LOCAL), F32),
        in_specs=[
            pl.BlockSpec((NB, LOCAL), lambda t: (t, 0)),
            pl.BlockSpec((1, NB), lambda t: (0, t)),
            pl.BlockSpec((2, NB, NB), lambda t: (0, t, 0)),
            pl.BlockSpec((2, NB, LOCAL), lambda t: (0, 0, 0)),
            pl.BlockSpec((3 * NB, NB), lambda t: (0, 0)),
        ],
        out_specs=pl.BlockSpec((NB, LOCAL), lambda t: (t, 0)),
        scratch_shapes=[
            pltpu.VMEM((2 * NB, LOCAL), jnp.bfloat16),
            pltpu.VMEM((2 * NB, LOCAL), jnp.bfloat16),
            pltpu.VMEM((3 * NB, NB), jnp.bfloat16),
            pltpu.VMEM((3 * NB, NB), jnp.bfloat16),
        ],
        compiler_params=pltpu.CompilerParams(vmem_limit_bytes=48 * 2**20),
        name="update",
    )(kernel, noise, a, b, f)


def body(kernel, noise):
    noise = noise.reshape(1, LOCAL)
    a, b, f = gather(kernel, noise)
    return update(kernel, noise, a, b, f)


def solution(mesh):
    return jax.shard_map(
        body,
        mesh=mesh,
        in_specs=(P("row", "col"), P("row")),
        out_specs=P("row", "col"),
        check_vma=False,
    )
```

time: 112 us -> 82.9 us (0.74)
  the two profiles are of different devices: /device:TPU:43 before, /device:TPU:115 now
where the time goes in v3:
time: 82.9 us; the launch traced here: 82.7 us
  Pallas kernels  82 us (99%)
    pallas_call x1, Pallas kernels, gather(): pl.pallas_call(gather_kernel, out_shape=(jax.ShapeDtypeStruct((2, LOCAL,...  66 us
    pallas_call x1, Pallas kernels, update(): pl.pallas_call(update_kernel, grid=(T,), out_shape=jax.ShapeDtypeStruct((...  16 us

profile of v3, /device:TPU:115, one launch (start us, length us, event | category | flops | bytes accessed | tf_op | source)
XLA Modules:
  0.0 82.7 jit_solution(13886484723258139593)
XLA Ops:
  0.0 0.7 reshape.3.noise_ref
  0.7 66.0 %gather_factor.1 = (f32[2,1280,256]{2,1,0:T(8,128)S(1)}, f32[2,256,1280]{2,1,0:T(8,128)S(1)}, f32[768,256]{1,0:T(8,128)S(1)}) custom-call(f32[1280,1280]{1,0:T(8,128)} %m_ref.1, f32[1,1280]{1,0:T(1,128)S(1)} %reshape.3.noise_ref), custom_call_target="tpu_custom_call" | custom-call | tf_op jit(solution)/shard_map/gather_factor/pallas_call | solution.py:449
  66.7 16.0 %update.1 = f32[1280,1280]{1,0:T(8,128)} custom-call(f32[1280,1280]{1,0:T(8,128)} %m_ref.1, f32[1,1280]{1,0:T(1,128)S(1)} %reshape.3.noise_ref, f32[2,1280,256]{2,1,0:T(8,128)S(1)} %get-tuple-element.8.a_ref, f32[2,256,1280]{2,1,0:T(8,128)S(1)} %get-tuple-element.9.b_ref, f32[768,256]{1,0:T(8,128)S(1)} %get-tuple-element.10.f_ref), custom_call_target="tpu_custom_call" | custom-call | tf_op jit(solution)/shard_map/update/pallas_call | solution.py:550

commit v4 on v3

v4 whole, which is shorter than its diff:
```python
import functools

import jax
import jax.numpy as jnp
from jax import lax
from jax.experimental import pallas as pl
from jax.experimental.pallas import tpu as pltpu
from jax.sharding import PartitionSpec as P

NB = 256
T = 5
LOCAL = NB * T
MESH = pl.DeviceIdType.MESH
HIGHEST = lax.Precision.HIGHEST
HIGH = lax.Precision.HIGH
F32 = jnp.float32

NA = 40
A_ROWS = LOCAL // NA
A_ONE = NA // 4
A_TURN = NA - A_ONE
HOP = 4
A_SLOTS = max(A_ONE + 7 * HOP, A_TURN + 4 * HOP)
NBC = 16
B_ROWS = NB // NBC
F_SLOT = 4
B_SLOTS = max(9, F_SLOT + 8)
PIECES = (
    ((0, 64, 128), (64, 64, 128), (128, 64, 256), (192, 64, 256))
    + tuple((NB + 64 * n, 64, 256) for n in range(4))
    + ((512, 64, 128), (576, 64, 128), (640, 64, 256), (704, 32, 256), (736, 32, 256))
)
STRIPS = 8
NF = len(PIECES)


def dot(a, b, dims, precision=HIGHEST):
    return lax.dot_general(a, b, (dims, ((), ())), precision=precision, preferred_element_type=F32)


def nn(a, b, precision=HIGHEST):
    return dot(a, b, ((1,), (0,)), precision)


def nt(a, b, precision=HIGHEST):
    return dot(a, b, ((1,), (1,)), precision)


def tn(a, b, precision=HIGHEST):
    return dot(a, b, ((0,), (0,)), precision)


def eliminate(rows, first):
    width = rows.shape[1]
    done = []
    for g in range(4):
        n = rows.shape[0]
        sub = lax.broadcasted_iota(jnp.int32, (n, 128), 0)
        at = first + 8 * g
        cols = [jnp.broadcast_to(rows[:, at + c : at + c + 1], (n, 128)) for c in range(8)]
        for j in range(8):
            inv = pltpu.reciprocal(cols[j][j : j + 1, :], approx=True)
            scale = jnp.where(sub > j, cols[j] * inv, 0.0)
            for c in range(j + 1, 8):
                cols[c] = cols[c] - scale * cols[c][j : j + 1, :]
            pivot = rows[j : j + 1, :]
            rows = jnp.concatenate(
                [rows[:, w : w + 128] - scale * pivot[:, w : w + 128] for w in range(0, width, 128)], axis=1
            )
        sub8 = lax.broadcasted_iota(jnp.int32, (8, 128), 0)
        diag = cols[0][:8]
        for j in range(1, 8):
            diag = jnp.where(sub8 == j, cols[j][:8], diag)
        root = lax.rsqrt(diag)
        done.append(rows[:8] * jnp.concatenate([root] * (width // 128), axis=1))
        rows = rows[8:]
    return jnp.concatenate(done, axis=0)


def factor_inverse(work, done=lambda k: None):
    following = None
    for k in range(8):
        r0 = 32 * k
        lo, hi = r0 // 128 * 128, NB + (r0 + 32 + 127) // 128 * 128
        rows = work[r0 : r0 + 32, lo:hi] if following is None else following
        rows = eliminate(rows, r0 - lo)
        work[r0 : r0 + 32, lo:hi] = rows
        done(k)
        if k == 7:
            break
        r1 = r0 + 32
        lo1, hi1 = r1 // 128 * 128, NB + (r1 + 32 + 127) // 128 * 128
        product = tn(rows[:, r1 - lo : r1 - lo + 32], rows)
        if hi1 > hi:
            product = jnp.concatenate([product, jnp.zeros((32, hi1 - hi), F32)], axis=1)
        following = work[r1 : r1 + 32, lo1:hi1] - product[:, lo1 - lo :]
        if k < 6:
            r2 = r1 + 32
            lo2 = r2 // 128 * 128
            product = tn(rows[:, lo2 - lo : NB - lo], rows[:, lo2 - lo :])
            work[r2:NB, lo2:hi] = work[r2:NB, lo2:hi] - product[r2 - lo2 :, :]


def identity():
    i0 = lax.broadcasted_iota(jnp.int32, (NB, NB), 0)
    i1 = lax.broadcasted_iota(jnp.int32, (NB, NB), 1)
    return i0 == i1


def gather_kernel(
    kernel_ref, noise_ref, a_out, b_out, f_out,
    a_buf, b_buf, f_buf, m_buf, work,
    a_recv, a_send, s_recv, s_send, b_recv, b_send, f_recv, f_send, m_recv, m_send, g_recv, g_send, local,
):
    p, q = lax.axis_index("row"), lax.axis_index("col")
    y, x, z, c = p // 4, p % 4, q // 2, q % 2
    rows_next = (y * 4 + (x + 1) % 4, (y + 1) % 4 * 4 + x, y * 4 + (x + 3) % 4, (y + 3) % 4 * 4 + x)
    z_next = ((z + 1) % 8, (z + 7) % 8)
    sib = (p, z * 2 + 1 - c)
    core0, core1 = c == 0, c == 1
    head = (p == 0) & (q == 0)
    a_source, b_source = z == 0, p < 2

    half = [pl.ds(k * NB, NB) for k in range(2)]
    side = [pl.ds(k * LOCAL, LOCAL) for k in range(2)]

    def a_load(s):
        return pltpu.make_async_copy(kernel_ref.at[:, pl.ds(0, NB)], a_buf.at[:, half[s]], local.at[0])

    def b_load(g, s):
        return pltpu.make_async_copy(kernel_ref.at[pl.ds(0, NB), :], b_buf.at[s, :, side[g]], local.at[1])

    def each_source(run_a, run_b):
        for s in range(2):
            @pl.when(a_source & (c == s))
            def _():
                run_a(s)

            for g in range(2):
                @pl.when((p == s) & (c == g))
                def _():
                    run_b(g, s)

    each_source(lambda s: a_load(s).start(), lambda g, s: b_load(g, s).start())
    for row in (0, 2 * NB):
        f_buf[row : row + 128, 128:] = jnp.zeros((128, 128), F32)

    barrier = pltpu.get_barrier_semaphore()
    peers = jnp.int32(7)

    def greet(device):
        pl.semaphore_signal(barrier, inc=1, device_id=device, device_id_type=MESH)

    for row in rows_next:
        greet((row, q))
    for level in z_next:
        greet((p, level * 2 + c))
    greet(sib)

    def greet_if(condition, devices):
        @pl.when(condition)
        def _():
            for device in devices:
                greet(device)

        return jnp.where(condition, len(devices), 0)

    peers += greet_if(head, [(0, 5), (0, 13), (1, 1)])
    peers += greet_if(((p == 0) & ((q == 5) | (q == 13))) | ((p == 1) & (q == 1)), [(0, 0)])
    peers += greet_if((p == 0) & (q == 5), [(0, 9)])
    peers += greet_if((p == 0) & (q == 9), [(0, 5)])
    peers += greet_if(core1 & (y == 0) & (x % 2 == 0), [((x + 2) % 4, q)])
    peers += greet_if(core1 & (y % 2 == 0), [((y + 2) % 4 * 4 + x, q)])

    each_source(lambda s: a_load(s).wait(), lambda g, s: b_load(g, s).wait())
    for s in range(2):
        @pl.when((p == s) & (q == s))
        def _():
            here = slice(s * NB, (s + 1) * NB)
            a_buf[:NB, here] = a_buf[:NB, here] + jnp.where(identity(), noise_ref[:, :NB], 0.0)

    pl.semaphore_wait(barrier, peers)

    def remote(src, dst, send_sem, recv_sem, device):
        return pltpu.make_async_remote_copy(
            src_ref=src, dst_ref=dst, send_sem=send_sem, recv_sem=recv_sem, device_id=device, device_id_type=MESH
        )

    def m_copy(which):
        return remote(a_buf.at[pl.ds(0, NB), half[which]], m_buf.at[which], m_send.at[which], m_recv.at[which], (0, 0))

    for which in range(2):
        @pl.when((p == 1) & (q == which))
        def _():
            m_copy(which).start()

    def a_ring(n, back):
        part = a_buf.at[pl.ds(n * A_ROWS, A_ROWS), :]
        return remote(part, part, a_send.at[back, n], a_recv.at[n], (p, z_next[back] * 2))

    def a_sib(n):
        part = a_buf.at[pl.ds(n * A_ROWS, A_ROWS), :]
        return remote(part, part, s_send.at[n], s_recv.at[n], sib)

    def a_join(s, i):
        part = a_buf.at[pl.ds(i * (LOCAL // 4), LOCAL // 4), half[s]]
        return remote(part, part, g_send.at[0, i], g_recv.at[0, i], sib)

    def b_plane(s, n, way):
        part = b_buf.at[s, pl.ds(n * B_ROWS, B_ROWS), :]
        return remote(part, part, b_send.at[way, s, n], b_recv.at[s, n], (rows_next[way], z * 2 + 1))

    def b_sib(s, n):
        part = b_buf.at[s, pl.ds(n * B_ROWS, B_ROWS), side[0]]
        return remote(part, part, b_send.at[4, s, n], b_recv.at[s, n], sib)

    def b_join(s, i):
        part = b_buf.at[s, pl.ds(i * (NB // 4), NB // 4), side[0]]
        return remote(part, part, g_send.at[1, i], g_recv.at[1, i], sib)

    a_hops = (z, 8 - z)

    def a_chunk(k, back):
        return jnp.where(k < A_ONE, 2 * k + back, A_ONE + k)

    def a_comes(k, back):
        return (k < A_ONE) | (a_hops[back] <= 4 - back)

    def a_more(k, back):
        return jnp.where(k < A_ONE, a_hops[back] < 7, a_hops[back] < 4 - back)

    def tree(s, k):
        dx, dy = (x + 4 - s) % 4, y
        u, v = ((dx, dy), (dy, (4 - dx) % 4), ((4 - dx) % 4, (4 - dy) % 4), ((4 - dy) % 4, dx))[k]
        hops = jnp.where(u == 0, 2, u) + jnp.minimum(v, 4 - v)
        sends = (
            (u == 2) | ((u == 1) & (v < 3)),
            (u == 1) & (v < 2),
            (u == 1) & (v >= 1),
            (v == 0) & ((u == 1) | (u == 2)),
        )
        return hops, [sends[(d - k) % 4] for d in range(4)]

    trees = {(s, k): tree(s, k) for s in range(2) for k in range(4)}

    def give_b(s):
        for i in range(4):
            b_join(s, i).start()

    each_source(
        lambda s: [a_join(s, i).start() for i in range(4)],
        lambda g, s: give_b(s) if g == 0 else None,
    )

    for s in range(2):
        @pl.when((p == s) & core1)
        def _():
            for i in range(4):
                b_join(s, i).wait_recv()
                for n in range(i * NBC // 4, (i + 1) * NBC // 4):
                    b_plane(s, n, n % 4).start()

    def a_first(k, carry):
        for back in range(2):
            a_ring(a_chunk(k, back), back).start()
        return carry

    @pl.when(a_source & core0)
    def _():
        a_join(1, 0).wait_recv()
        a_join(1, 1).wait_recv()
        lax.fori_loop(0, A_ONE, a_first, 0)
        a_join(1, 2).wait_recv()
        lax.fori_loop(A_ONE, 2 * A_ONE, a_first, 0)
        a_join(1, 3).wait_recv()
        lax.fori_loop(2 * A_ONE, A_TURN, a_first, 0)

    top = core1 & (p == 0)
    edge = core1 & (y == 0)
    every, large, strips = range(NF), range(STRIPS), range(STRIPS, NF)
    f_ways = [(head, (0, k), every) for k in (5, 13, 1)]
    f_ways += [(top & (z == 2), (0, 9), strips)] + [(top & (z == 2), (0, k), every) for k in (7, 3)] + [(top & (z == 6), (0, k), every) for k in (11, 15)]
    f_ways += [(top & (z == 5), (0, 9), large)]
    f_ways += [(top, (2, q), strips), (top, (1, q), every), (top, (3, q), every), (edge & (x == 1), (2, q), large)]
    f_ways += [(edge, (8 + x, q), strips), (edge, (4 + x, q), every), (edge, (12 + x, q), every)]
    f_ways += [(core1 & (y == 1), (8 + x, q), large)]
    f_ways += [(core1 & ((p != 0) | (q != 1)), sib, every)]
    F_HEAD = 3

    def f_copy(n, way, device):
        row, size, width = PIECES[n]
        part = f_buf.at[pl.ds(row, size), pl.ds(0, width)]
        return remote(part, part, f_send.at[way, n], f_recv.at[n], device)

    def pass_f(n):
        f_copy(n, 0, sib).wait_recv()
        for way in range(F_HEAD, len(f_ways)):
            if n in f_ways[way][2]:
                @pl.when(f_ways[way][0])
                def _():
                    f_copy(n, way, f_ways[way][1]).start()

    def far(v):
        return jnp.where(v == 0, 0, jnp.where(v == 2, 2, 1))

    f_slot = F_SLOT + far(x) + far(y) + jnp.where(z == 0, 0, jnp.where(z == 4, 3, jnp.where(z % 4 == 2, 1, 2)))

    def pass_a(slot, carry):
        @pl.when(core0 & (z != 0))
        def _():
            for back in range(2):
                m = slot - HOP * a_hops[back]
                k = (m + 3 * A_TURN) % A_TURN
                n = a_chunk(k, back)

                @pl.when((m >= 0) & (m < A_TURN) & a_comes(k, back))
                def _():
                    a_ring(n, back).wait_recv()

                    @pl.when(a_more(k, back))
                    def _():
                        a_ring(n, back).start()

                    a_sib(n).start()

        return carry

    def pass_b(slot, carry):
        @pl.when(core1)
        def _():
            for (s, k), (hops, sends) in trees.items():
                m = slot - hops
                n = 4 * ((m + NBC) % (NBC // 4)) + k

                @pl.when((p != s) & (m >= 0) & (m < NBC // 4))
                def _():
                    b_plane(s, n, 0).wait_recv()
                    for way in range(4):
                        @pl.when(sends[way])
                        def _():
                            b_plane(s, n, way).start()

                    b_sib(s, n).start()

            @pl.when(slot == f_slot)
            def _():
                for n in large:
                    pass_f(n)

        return carry

    lax.fori_loop(0, A_SLOTS, pass_a, 0)
    lax.fori_loop(0, B_SLOTS, pass_b, 0)

    def a_wait_sib():
        @pl.when(a_source)
        def _():
            for i in range(4):
                a_join(0, i).wait_recv()

        @pl.when(jnp.logical_not(a_source))
        def _():
            def wait(n, carry):
                a_sib(n).wait_recv()
                return carry

            lax.fori_loop(0, NA, wait, 0)

    def b_wait_sib(n, carry):
        for s in range(2):
            @pl.when(p != s)
            def _():
                b_sib(s, n).wait_recv()

        return carry

    a_store = pltpu.make_async_copy(a_buf, a_out, local.at[0])

    def b_store(g):
        return pltpu.make_async_copy(b_buf.at[:, :, side[g]], b_out, local.at[1])

    f_store = pltpu.make_async_copy(f_buf, f_out, local.at[2])

    @pl.when(head)
    def _():
        eye = jnp.where(identity(), 1.0, 0.0)

        def put(first, last, value):
            f_buf[first:last, :] = value
            for n in range(NF):
                if first <= PIECES[n][0] < last:
                    for way in range(F_HEAD):
                        f_copy(n, way, f_ways[way][1]).start()

        work[:, :NB] = a_buf[:NB, :NB]
        work[:, NB:] = eye
        factor_inverse(work)
        put(0, NB, work[:, NB:])
        m_copy(0).wait_recv()
        l10 = nt(m_buf[0], work[:, NB:])
        put(NB, 2 * NB, l10)
        m_copy(1).wait_recv()
        work[:, :NB] = m_buf[1] - nt(l10, l10)
        work[:, NB:] = eye

        def strip(k):
            last = 32 * (k + 1)
            for start, size, _ in PIECES:
                if start - 2 * NB + size == last:
                    put(start, start + size, work[last - size : last, NB:])

        factor_inverse(work, strip)
        lax.fori_loop(0, NBC, b_wait_sib, 0)
        a_store.start()
        b_store(0).start()

    @pl.when(core0 & jnp.logical_not(head))
    def _():
        a_store.start()
        lax.fori_loop(0, NBC, b_wait_sib, 0)
        b_store(0).start()
        for n in range(NF):
            f_copy(n, 0, sib).wait_recv()

    @pl.when(core1)
    def _():
        b_store(1).start()
        a_wait_sib()
        a_store.start()
        for n in strips:
            pass_f(n)

    f_store.start()

    each_source(
        lambda s: [a_join(s, i).wait_send() for i in range(4)],
        lambda g, s: [b_join(s, i).wait_send() for i in range(4)] if g == 0 else None,
    )

    def finish_a(k, carry):
        for back in range(2):
            n = a_chunk(k, back)

            @pl.when(core0 & (a_source | (a_comes(k, back) & a_more(k, back))))
            def _():
                a_ring(n, back).wait_send()

            @pl.when(core0 & (z != 0) & a_comes(k, back))
            def _():
                a_sib(n).wait_send()

        return carry

    lax.fori_loop(0, A_TURN, finish_a, 0)

    def finish_b(m, carry):
        @pl.when(core1)
        def _():
            for (s, k), (hops, sends) in trees.items():
                @pl.when(p == s)
                def _():
                    b_plane(s, 4 * m + k, k).wait_send()

                @pl.when(p != s)
                def _():
                    for way in range(4):
                        @pl.when(sends[way])
                        def _():
                            b_plane(s, 4 * m + k, way).wait_send()

                    b_sib(s, 4 * m + k).wait_send()

        return carry

    lax.fori_loop(0, NBC // 4, finish_b, 0)

    for n in range(NF):
        for way, (sends, device, pieces) in enumerate(f_ways):
            if n in pieces:
                @pl.when(sends)
                def _():
                    f_copy(n, way, device).wait_send()

    for which in range(2):
        @pl.when((p == 1) & (q == which))
        def _():
            m_copy(which).wait_send()

    a_store.wait()
    for g in range(2):
        @pl.when(c == g)
        def _():
            b_store(g).wait()

    f_store.wait()


def gather(kernel, noise):
    return pl.pallas_call(
        gather_kernel,
        out_shape=(
            jax.ShapeDtypeStruct((LOCAL, 2 * NB), F32),
            jax.ShapeDtypeStruct((2, NB, LOCAL), F32),
            jax.ShapeDtypeStruct((3 * NB, NB), F32),
        ),
        in_specs=[pl.BlockSpec(memory_space=pl.ANY), pl.BlockSpec(memory_space=pltpu.VMEM)],
        out_specs=[pl.BlockSpec(memory_space=pl.ANY)] * 3,
        scratch_shapes=[
            pltpu.VMEM((LOCAL, 2 * NB), F32),
            pltpu.VMEM((2, NB, 2 * LOCAL), F32),
            pltpu.VMEM((3 * NB, NB), F32),
            pltpu.VMEM((2, NB, NB), F32),
            pltpu.VMEM((NB, 2 * NB), F32),
            pltpu.SemaphoreType.DMA((NA,)),
            pltpu.SemaphoreType.DMA((2, NA)),
            pltpu.SemaphoreType.DMA((NA,)),
            pltpu.SemaphoreType.DMA((NA,)),
            pltpu.SemaphoreType.DMA((2, NBC)),
            pltpu.SemaphoreType.DMA((5, 2, NBC)),
            pltpu.SemaphoreType.DMA((NF,)),
            pltpu.SemaphoreType.DMA((18, NF)),
            pltpu.SemaphoreType.DMA((2,)),
            pltpu.SemaphoreType.DMA((2,)),
            pltpu.SemaphoreType.DMA((2, 4)),
            pltpu.SemaphoreType.DMA((2, 4)),
            pltpu.SemaphoreType.DMA((3,)),
        ],
        compiler_params=pltpu.CompilerParams(
            collective_id=0, has_side_effects=True, vmem_limit_bytes=48 * 2**20
        ),
        name="gather_factor",
    )(kernel, noise)


def split(value):
    high = value.astype(jnp.bfloat16)
    return high, (value - high.astype(F32)).astype(jnp.bfloat16)


def left(parts):
    return jnp.concatenate([parts[0], parts[0], parts[1]], axis=1)


def below(parts):
    return jnp.concatenate([parts[0], parts[1], parts[0]], axis=0)


def beside(parts):
    return jnp.concatenate([parts[0], parts[1], parts[0]], axis=1)


def product(a, b, dims=((1,), (0,))):
    return lax.dot_general(a, b, (dims, ((), ())), preferred_element_type=F32)


NT = ((1,), (1,))


def update_kernel(
    m_ref, noise_ref, a_ref, b_ref, f_ref, out_ref,
    m_buf, a_buf, b_buf, f_buf, rows, cols, m_sem, a_sem, b_sem, f_sem, out_sem,
):
    p, q = lax.axis_index("row"), lax.axis_index("col")
    strip = [pl.ds(t * NB, NB) for t in range(T)]
    f_load = pltpu.make_async_copy(f_ref, f_buf, f_sem)
    b_load = pltpu.make_async_copy(b_ref, b_buf, b_sem)
    a_load = pltpu.make_async_copy(a_ref, a_buf, a_sem)
    m_load = [pltpu.make_async_copy(m_ref.at[strip[t]], m_buf.at[strip[t]], m_sem.at[t]) for t in range(T)]
    store = [pltpu.make_async_copy(m_buf.at[strip[t]], out_ref.at[strip[t]], out_sem.at[t]) for t in range(T)]
    f_load.start()
    a_load.start()
    b_load.start()
    for t in range(T):
        m_load[t].start()

    f_load.wait()
    x0, l10, x1 = [split(f_buf[k * NB : (k + 1) * NB, :]) for k in range(3)]
    a_load.wait()
    row0 = product(left(split(a_buf[:, :NB])), beside(x0), NT)
    row0_parts = split(row0)
    row1 = product(left(split(a_buf[:, NB:] - product(left(row0_parts), beside(l10), NT))), beside(x1), NT)
    row1_parts = split(row1)
    for at, value in enumerate((row0_parts[0], row1_parts[0], row0_parts[1], row1_parts[1])):
        rows[:, at * NB : (at + 1) * NB] = value
    b_load.wait()
    col0 = split(product(left(x0), below(split(b_buf[0]))))
    col1 = split(product(left(x1), below(split(b_buf[1] - product(left(l10), below(col0))))))
    for at, value in enumerate((col0[0], col1[0], col0[1], col1[1])):
        cols[at * NB : (at + 1) * NB, :] = value

    for t in range(T):
        m_load[t].wait()
    i0 = lax.broadcasted_iota(jnp.int32, (NB, NB), 0)
    i1 = lax.broadcasted_iota(jnp.int32, (NB, NB), 1)
    for col in range(T):
        at = slice(col * NB, (col + 1) * NB)

        def blocks():
            high, low = slice(0, 2 * NB), slice(2 * NB, 4 * NB)
            u = jnp.concatenate([rows[col * NB :, high], rows[col * NB :, high], rows[col * NB :, low]], axis=1)
            v = jnp.concatenate([cols[high, at], cols[low, at], cols[high, at]], axis=0)
            value = m_buf[col * NB :, at] - product(u, v)
            first = value[:NB] + jnp.where((i0 == i1) & (p == q), noise_ref[:, at], 0.0)
            m_buf[at, at] = jnp.where(p >= q, first, m_buf[at, at])
            if col < T - 1:
                m_buf[(col + 1) * NB :, at] = value[NB:]

        if col > 0:
            blocks()
        else:
            pl.when(q >= 2)(blocks)

            @pl.when(q < 2)
            def _():
                panel = jnp.where(q == 0, row0, row1)
                first = jnp.where((p == q) & (i0 < i1), 0.0, panel[:NB])
                m_buf[at, at] = jnp.where(p >= q, first, m_buf[at, at])
                m_buf[NB:, at] = panel[NB:]

        store[col].start()
    for t in range(T):
        store[t].wait()


def update(kernel, noise, a, b, f):
    whole = pl.BlockSpec(memory_space=pl.ANY)
    return pl.pallas_call(
        update_kernel,
        out_shape=jax.ShapeDtypeStruct((LOCAL, LOCAL), F32),
        in_specs=[whole, pl.BlockSpec(memory_space=pltpu.VMEM), whole, whole, whole],
        out_specs=whole,
        scratch_shapes=[
            pltpu.VMEM((LOCAL, LOCAL), F32),
            pltpu.VMEM((LOCAL, 2 * NB), F32),
            pltpu.VMEM((2, NB, LOCAL), F32),
            pltpu.VMEM((3 * NB, NB), F32),
            pltpu.VMEM((LOCAL, 4 * NB), jnp.bfloat16),
            pltpu.VMEM((4 * NB, LOCAL), jnp.bfloat16),
            pltpu.SemaphoreType.DMA((T,)),
            pltpu.SemaphoreType.DMA,
            pltpu.SemaphoreType.DMA,
            pltpu.SemaphoreType.DMA,
            pltpu.SemaphoreType.DMA((T,)),
        ],
        compiler_params=pltpu.CompilerParams(vmem_limit_bytes=48 * 2**20),
        name="update",
    )(kernel, noise, a, b, f)


def body(kernel, noise):
    noise = noise.reshape(1, LOCAL)
    a, b, f = gather(kernel, noise)
    return update(kernel, noise, a, b, f)


def solution(mesh):
    return jax.shard_map(
        body,
        mesh=mesh,
        in_specs=(P("row", "col"), P("row")),
        out_specs=P("row", "col"),
        check_vma=False,
    )
```

time: 82.9 us -> 76.4 us (0.922)
  the two profiles are of different devices: /device:TPU:115 before, /device:TPU:141 now
where the time goes in v4:
time: 76.4 us; the launch traced here: 75.5 us
  Pallas kernels  74.6 us (98%)
    pallas_call x1, Pallas kernels, gather(): pl.pallas_call(gather_kernel, out_shape=(jax.ShapeDtypeStruct((LOCAL, 2 *...  63.6 us
    pallas_call x1, Pallas kernels, update(): pl.pallas_call(update_kernel, out_shape=jax.ShapeDtypeStruct((LOCAL, LOCA...  11.1 us

profile of v4, /device:TPU:141, one launch (start us, length us, event | category | flops | bytes accessed | tf_op | source)
XLA Modules:
  0.0 75.5 jit_solution(11364006518229447637)
XLA Ops:
  0.0 0.7 reshape.3.noise_ref
  0.7 63.6 %gather_factor.1 = (f32[1280,512]{1,0:T(8,128)S(1)}, f32[2,256,1280]{2,1,0:T(8,128)S(1)}, f32[768,256]{1,0:T(8,128)S(1)}) custom-call(f32[1280,1280]{1,0:T(8,128)} %m_ref.1, f32[1,1280]{1,0:T(1,128)S(1)} %reshape.3.noise_ref), custom_call_target="tpu_custom_call" | custom-call | tf_op jit(solution)/shard_map/gather_factor/pallas_call | solution.py:499
  64.3 11.1 %update.1 = f32[1280,1280]{1,0:T(8,128)} custom-call(f32[1280,1280]{1,0:T(8,128)} %m_ref.1, f32[1,1280]{1,0:T(1,128)S(1)} %reshape.3.noise_ref, f32[1280,512]{1,0:T(8,128)S(1)} %get-tuple-element.8.a_ref, f32[2,256,1280]{2,1,0:T(8,128)S(1)} %get-tuple-element.9.b_ref, f32[768,256]{1,0:T(8,128)S(1)} %get-tuple-element.10.f_ref), custom_call_target="tpu_custom_call" | custom-call | tf_op jit(solution)/shard_map/update/pallas_call | solution.py:627

commit v5 on v4

--- a/solution.py
+++ b/solution.py
@@ -110,7 +110,7 @@
 def gather_kernel(
     kernel_ref, noise_ref, a_out, b_out, f_out,
     a_buf, b_buf, f_buf, m_buf, work,
-    a_recv, a_send, s_recv, s_send, b_recv, b_send, f_recv, f_send, m_recv, m_send, g_recv, g_send, local,
+    a_recv, a_send, s_recv, s_send, b_recv, b_send, f_recv, f_send, m_recv, m_send, g_recv, g_send, t_recv, t_send, h_recv, local,
 ):
     p, q = lax.axis_index("row"), lax.axis_index("col")
     y, x, z, c = p // 4, p % 4, q // 2, q % 2
@@ -196,23 +196,31 @@
 
     def a_ring(n, back):
         part = a_buf.at[pl.ds(n * A_ROWS, A_ROWS), :]
-        return remote(part, part, a_send.at[back, n], a_recv.at[n], (p, z_next[back] * 2))
-
-    def a_sib(n):
-        part = a_buf.at[pl.ds(n * A_ROWS, A_ROWS), :]
-        return remote(part, part, s_send.at[n], s_recv.at[n], sib)
+        return remote(part, part, a_send.at[back, jnp.where(n < 2 * A_ONE, 0, 1)], a_recv.at[n], (p, z_next[back] * 2))
+
+    def a_sib(first, count):
+        part = a_buf.at[pl.ds(first * A_ROWS, count * A_ROWS), :]
+        return remote(part, part, s_send, s_recv, sib)
+
+    def a_sent(back, group):
+        part = a_buf.at[pl.ds(0, (A_ONE, A_TURN - A_ONE)[group] * A_ROWS), :]
+        return remote(part, part, a_send.at[back, group], a_recv.at[0], (p, z_next[back] * 2))
 
     def a_join(s, i):
         part = a_buf.at[pl.ds(i * (LOCAL // 4), LOCAL // 4), half[s]]
         return remote(part, part, g_send.at[0, i], g_recv.at[0, i], sib)
 
-    def b_plane(s, n, way):
+    def b_plane(s, n, k, way):
         part = b_buf.at[s, pl.ds(n * B_ROWS, B_ROWS), :]
-        return remote(part, part, b_send.at[way, s, n], b_recv.at[s, n], (rows_next[way], z * 2 + 1))
-
-    def b_sib(s, n):
-        part = b_buf.at[s, pl.ds(n * B_ROWS, B_ROWS), side[0]]
-        return remote(part, part, b_send.at[4, s, n], b_recv.at[s, n], sib)
+        return remote(part, part, b_send.at[way, s, k], b_recv.at[s, n], (rows_next[way], z * 2 + 1))
+
+    def b_sent(s, k, way):
+        part = b_buf.at[s, pl.ds(0, NB // 4), :]
+        return remote(part, part, b_send.at[way, s, k], b_recv.at[s, 0], (rows_next[way], z * 2 + 1))
+
+    def b_sib(s, first, count):
+        part = b_buf.at[s, pl.ds(first * (NB // 4), count * (NB // 4)), side[0]]
+        return remote(part, part, t_send.at[s], t_recv.at[s], sib)
 
     def b_join(s, i):
         part = b_buf.at[s, pl.ds(i * (NB // 4), NB // 4), side[0]]
@@ -242,6 +250,13 @@
         return hops, [sends[(d - k) % 4] for d in range(4)]
 
     trees = {(s, k): tree(s, k) for s in range(2) for k in range(4)}
+    b_last = []
+    for s in range(2):
+        last = trees[s, 0][0]
+        for k in range(1, 4):
+            last = jnp.where(trees[s, k][0] > last, trees[s, k][0], last)
+        b_last.append(last)
+
 
     def give_b(s):
         for i in range(4):
@@ -258,7 +273,7 @@
             for i in range(4):
                 b_join(s, i).wait_recv()
                 for n in range(i * NBC // 4, (i + 1) * NBC // 4):
-                    b_plane(s, n, n % 4).start()
+                    b_plane(s, n, n % 4, n % 4).start()
 
     def a_first(k, carry):
         for back in range(2):
@@ -290,7 +305,14 @@
     def f_copy(n, way, device):
         row, size, width = PIECES[n]
         part = f_buf.at[pl.ds(row, size), pl.ds(0, width)]
-        return remote(part, part, f_send.at[way, n], f_recv.at[n], device)
+        if way == len(f_ways) - 1:
+            return remote(part, part, f_send.at[way], h_recv, device)
+        return remote(part, part, f_send.at[way], f_recv.at[n], device)
+
+    def f_whole(way, pieces):
+        part = f_buf.at[pl.ds(0, sum(PIECES[n][1] * PIECES[n][2] for n in pieces) // NB), :]
+        return remote(part, part, f_send.at[way], h_recv, sib)
+
 
     def pass_f(n):
         f_copy(n, 0, sib).wait_recv()
@@ -321,7 +343,7 @@
                     def _():
                         a_ring(n, back).start()
 
-                    a_sib(n).start()
+                    a_sib(n, 1).start()
 
         return carry
 
@@ -334,13 +356,18 @@
 
                 @pl.when((p != s) & (m >= 0) & (m < NBC // 4))
                 def _():
-                    b_plane(s, n, 0).wait_recv()
+                    b_plane(s, n, k, 0).wait_recv()
                     for way in range(4):
                         @pl.when(sends[way])
                         def _():
-                            b_plane(s, n, way).start()
-
-                    b_sib(s, n).start()
+                            b_plane(s, n, k, way).start()
+
+            for s in range(2):
+                m = slot - b_last[s]
+
+                @pl.when((p != s) & (m >= 0) & (m < 4))
+                def _():
+                    b_sib(s, (m + NBC) % 4, 1).start()
 
             @pl.when(slot == f_slot)
             def _():
@@ -360,19 +387,13 @@
 
         @pl.when(jnp.logical_not(a_source))
         def _():
-            def wait(n, carry):
-                a_sib(n).wait_recv()
-                return carry
-
-            lax.fori_loop(0, NA, wait, 0)
-
-    def b_wait_sib(n, carry):
+            a_sib(0, NA).wait_recv()
+
+    def b_wait_sib():
         for s in range(2):
             @pl.when(p != s)
             def _():
-                b_sib(s, n).wait_recv()
-
-        return carry
+                b_sib(s, 0, 4).wait_recv()
 
     a_store = pltpu.make_async_copy(a_buf, a_out, local.at[0])
 
@@ -410,25 +431,25 @@
                     put(start, start + size, work[last - size : last, NB:])
 
         factor_inverse(work, strip)
-        lax.fori_loop(0, NBC, b_wait_sib, 0)
+        b_wait_sib()
         a_store.start()
         b_store(0).start()
 
     @pl.when(core0 & jnp.logical_not(head))
     def _():
         a_store.start()
-        lax.fori_loop(0, NBC, b_wait_sib, 0)
+        b_wait_sib()
         b_store(0).start()
-        for n in range(NF):
-            f_copy(n, 0, sib).wait_recv()
+        f_whole(0, every).wait_recv()
 
     @pl.when(core1)
     def _():
         b_store(1).start()
+        for n in strips:
+            pass_f(n)
+
         a_wait_sib()
         a_store.start()
-        for n in strips:
-            pass_f(n)
 
     f_store.start()
 
@@ -437,49 +458,33 @@
         lambda g, s: [b_join(s, i).wait_send() for i in range(4)] if g == 0 else None,
     )
 
-    def finish_a(k, carry):
-        for back in range(2):
-            n = a_chunk(k, back)
-
+    for back in range(2):
+        for group, k in enumerate((0, A_ONE)):
             @pl.when(core0 & (a_source | (a_comes(k, back) & a_more(k, back))))
             def _():
-                a_ring(n, back).wait_send()
-
-            @pl.when(core0 & (z != 0) & a_comes(k, back))
+                a_sent(back, group).wait_send()
+
+    @pl.when(core0 & (z != 0))
+    def _():
+        a_sib(0, NA).wait_send()
+
+    for (s, k), (hops, sends) in trees.items():
+        for way in range(4):
+            mine = jnp.where(p == s, way == k, sends[way])
+
+            @pl.when(core1 & mine)
             def _():
-                a_sib(n).wait_send()
-
-        return carry
-
-    lax.fori_loop(0, A_TURN, finish_a, 0)
-
-    def finish_b(m, carry):
-        @pl.when(core1)
-        def _():
-            for (s, k), (hops, sends) in trees.items():
-                @pl.when(p == s)
-                def _():
-                    b_plane(s, 4 * m + k, k).wait_send()
-
-                @pl.when(p != s)
-                def _():
-                    for way in range(4):
-                        @pl.when(sends[way])
-                        def _():
-                            b_plane(s, 4 * m + k, way).wait_send()
-
-                    b_sib(s, 4 * m + k).wait_send()
-
-        return carry
-
-    lax.fori_loop(0, NBC // 4, finish_b, 0)
-
-    for n in range(NF):
-        for way, (sends, device, pieces) in enumerate(f_ways):
-            if n in pieces:
-                @pl.when(sends)
-                def _():
-                    f_copy(n, way, device).wait_send()
+                b_sent(s, k, way).wait_send()
+
+    for s in range(2):
+        @pl.when(core1 & (p != s))
+        def _():
+            b_sib(s, 0, 4).wait_send()
+
+    for way, (sends, device, pieces) in enumerate(f_ways):
+        @pl.when(sends)
+        def _():
+            f_whole(way, pieces).wait_send()
 
     for which in range(2):
         @pl.when((p == 1) & (q == which))
@@ -512,17 +517,20 @@
             pltpu.VMEM((2, NB, NB), F32),
             pltpu.VMEM((NB, 2 * NB), F32),
             pltpu.SemaphoreType.DMA((NA,)),
-            pltpu.SemaphoreType.DMA((2, NA)),
-            pltpu.SemaphoreType.DMA((NA,)),
-            pltpu.SemaphoreType.DMA((NA,)),
+            pltpu.SemaphoreType.DMA((2, 2)),
+            pltpu.SemaphoreType.DMA,
+            pltpu.SemaphoreType.DMA,
             pltpu.SemaphoreType.DMA((2, NBC)),
-            pltpu.SemaphoreType.DMA((5, 2, NBC)),
+            pltpu.SemaphoreType.DMA((4, 2, 4)),
             pltpu.SemaphoreType.DMA((NF,)),
-            pltpu.SemaphoreType.DMA((18, NF)),
+            pltpu.SemaphoreType.DMA((18,)),
             pltpu.SemaphoreType.DMA((2,)),
             pltpu.SemaphoreType.DMA((2,)),
             pltpu.SemaphoreType.DMA((2, 4)),
             pltpu.SemaphoreType.DMA((2, 4)),
+            pltpu.SemaphoreType.DMA((2,)),
+            pltpu.SemaphoreType.DMA((2,)),
+            pltpu.SemaphoreType.DMA,
             pltpu.SemaphoreType.DMA((3,)),
         ],
         compiler_params=pltpu.CompilerParams(

time: 76.4 us -> 67.5 us (0.88)
  Pallas kernels: 74.6 us -> 66.4 us
    pallas_call x1, Pallas kernels: 63.6 us -> 55.4 us  [gather(): pl.pallas_call(gather_kernel, out_shape=(jax.ShapeDtypeStruct((LOCAL, 2 *...]
where the time goes in v5:
time: 67.5 us; the launch traced here: 67.3 us
  Pallas kernels  66.4 us (98%)
  local copies, waits for them, and re-layouts  0.7 us (1%)
    pallas_call x1, Pallas kernels, gather(): pl.pallas_call(gather_kernel, out_shape=(jax.ShapeDtypeStruct((LOCAL, 2 *...  55.4 us
    pallas_call x1, Pallas kernels, update(): pl.pallas_call(update_kernel, out_shape=jax.ShapeDtypeStruct((LOCAL, LOCA...  11.1 us

profile of v5, /device:TPU:141, one launch (start us, length us, event | category | flops | bytes accessed | tf_op | source)
XLA Modules:
  0.0 67.3 jit_solution(14050024237763521034)
XLA Ops:
  0.0 0.7 %reshape.3.noise_ref = f32[1,1280]{1,0:T(1,128)S(1)} reshape(f32[1280]{0:T(1024)} %param.3) | data formatting | bytes 10240 | tf_op jit(solution)/shard_map/reshape | solution.py:659
  0.7 55.4 %gather_factor.1 = (f32[1280,512]{1,0:T(8,128)S(1)}, f32[2,256,1280]{2,1,0:T(8,128)S(1)}, f32[768,256]{1,0:T(8,128)S(1)}) custom-call(f32[1280,1280]{1,0:T(8,128)} %m_ref.1, f32[1,1280]{1,0:T(1,128)S(1)} %reshape.3.noise_ref), custom_call_target="tpu_custom_call" | custom-call | tf_op jit(solution)/shard_map/gather_factor/pallas_call | solution.py:504
  56.1 11.1 %update.1 = f32[1280,1280]{1,0:T(8,128)} custom-call(f32[1280,1280]{1,0:T(8,128)} %m_ref.1, f32[1,1280]{1,0:T(1,128)S(1)} %reshape.3.noise_ref, f32[1280,512]{1,0:T(8,128)S(1)} %get-tuple-element.8.a_ref, f32[2,256,1280]{2,1,0:T(8,128)S(1)} %get-tuple-element.9.b_ref, f32[768,256]{1,0:T(8,128)S(1)} %get-tuple-element.10.f_ref), custom_call_target="tpu_custom_call" | custom-call | tf_op jit(solution)/shard_map/update/pallas_call | solution.py:635

commit v6 on v5

--- a/solution.py
+++ b/solution.py
@@ -15,15 +15,15 @@
 HIGH = lax.Precision.HIGH
 F32 = jnp.float32
 
-NA = 40
+NA = 20
 A_ROWS = LOCAL // NA
 A_ONE = NA // 4
 A_TURN = NA - A_ONE
-HOP = 4
+HOP = 3
 A_SLOTS = max(A_ONE + 7 * HOP, A_TURN + 4 * HOP)
 NBC = 16
 B_ROWS = NB // NBC
-F_SLOT = 4
+F_SLOT = 3
 B_SLOTS = max(9, F_SLOT + 8)
 PIECES = (
     ((0, 64, 128), (64, 64, 128), (128, 64, 256), (192, 64, 256))
@@ -110,7 +110,7 @@
 def gather_kernel(
     kernel_ref, noise_ref, a_out, b_out, f_out,
     a_buf, b_buf, f_buf, m_buf, work,
-    a_recv, a_send, s_recv, s_send, b_recv, b_send, f_recv, f_send, m_recv, m_send, g_recv, g_send, t_recv, t_send, h_recv, local,
+    a_recv, a_send, s_recv, s_send, b_recv, b_send, f_recv, f_send, m_recv, m_send, g_recv, g_send, o_recv, r_recv, t_recv, t_send, h_recv, local,
 ):
     p, q = lax.axis_index("row"), lax.axis_index("col")
     y, x, z, c = p // 4, p % 4, q // 2, q % 2
@@ -165,8 +165,14 @@
 
         return jnp.where(condition, len(devices), 0)
 
-    peers += greet_if(head, [(0, 5), (0, 13), (1, 1)])
-    peers += greet_if(((p == 0) & ((q == 5) | (q == 13))) | ((p == 1) & (q == 1)), [(0, 0)])
+    peers += greet_if(a_source & core1, [(p, 2), (p, 14)])
+    peers += greet_if(core0 & ((z == 1) | (z == 7)), [(p, 1)])
+    peers += greet_if(b_source & core0, [(row, z * 2 + 1) for row in rows_next])
+    for s in range(2):
+        near = ((y == 0) & ((x + 4 - s) % 2 == 1)) | ((x == s) & (y % 2 == 1))
+        peers += greet_if(core1 & near, [(s, z * 2)])
+    peers += greet_if(head, [(0, 5), (0, 13)])
+    peers += greet_if((p == 0) & ((q == 5) | (q == 13)), [(0, 0)])
     peers += greet_if((p == 0) & (q == 5), [(0, 9)])
     peers += greet_if((p == 0) & (q == 9), [(0, 5)])
     peers += greet_if(core1 & (y == 0) & (x % 2 == 0), [((x + 2) % 4, q)])
@@ -206,9 +212,25 @@
         part = a_buf.at[pl.ds(0, (A_ONE, A_TURN - A_ONE)[group] * A_ROWS), :]
         return remote(part, part, a_send.at[back, group], a_recv.at[0], (p, z_next[back] * 2))
 
-    def a_join(s, i):
-        part = a_buf.at[pl.ds(i * (LOCAL // 4), LOCAL // 4), half[s]]
-        return remote(part, part, g_send.at[0, i], g_recv.at[0, i], sib)
+    def a_half(s, n, back):
+        part = a_buf.at[pl.ds(n * A_ROWS, A_ROWS), half[s]]
+        return remote(part, part, g_send.at[back], (a_recv, o_recv)[s].at[n], (p, z_next[back] * 2))
+
+    def a_gave(s, back):
+        part = a_buf.at[pl.ds(0, A_TURN * A_ROWS), half[s]]
+        return remote(part, part, g_send.at[back], g_recv, (p, z_next[back] * 2))
+
+    def a_join(s):
+        part = a_buf.at[:, half[s]]
+        return remote(part, part, g_send.at[2], g_recv, sib)
+
+    def b_half(g, s, n, k):
+        part = b_buf.at[s, pl.ds(n * B_ROWS, B_ROWS), side[g]]
+        return remote(part, part, g_send.at[3], (r_recv, b_recv)[g].at[s, n], (rows_next[k], z * 2 + 1))
+
+    def b_gave(g, s):
+        part = b_buf.at[s, :, side[g]]
+        return remote(part, part, g_send.at[3], g_recv, sib)
 
     def b_plane(s, n, k, way):
         part = b_buf.at[s, pl.ds(n * B_ROWS, B_ROWS), :]
@@ -221,10 +243,6 @@
     def b_sib(s, first, count):
         part = b_buf.at[s, pl.ds(first * (NB // 4), count * (NB // 4)), side[0]]
         return remote(part, part, t_send.at[s], t_recv.at[s], sib)
-
-    def b_join(s, i):
-        part = b_buf.at[s, pl.ds(i * (NB // 4), NB // 4), side[0]]
-        return remote(part, part, g_send.at[1, i], g_recv.at[1, i], sib)
 
     a_hops = (z, 8 - z)
 
@@ -258,37 +276,25 @@
         b_last.append(last)
 
 
-    def give_b(s):
-        for i in range(4):
-            b_join(s, i).start()
-
-    each_source(
-        lambda s: [a_join(s, i).start() for i in range(4)],
-        lambda g, s: give_b(s) if g == 0 else None,
-    )
-
-    for s in range(2):
-        @pl.when((p == s) & core1)
-        def _():
-            for i in range(4):
-                b_join(s, i).wait_recv()
-                for n in range(i * NBC // 4, (i + 1) * NBC // 4):
-                    b_plane(s, n, n % 4, n % 4).start()
-
-    def a_first(k, carry):
-        for back in range(2):
-            a_ring(a_chunk(k, back), back).start()
-        return carry
-
-    @pl.when(a_source & core0)
-    def _():
-        a_join(1, 0).wait_recv()
-        a_join(1, 1).wait_recv()
-        lax.fori_loop(0, A_ONE, a_first, 0)
-        a_join(1, 2).wait_recv()
-        lax.fori_loop(A_ONE, 2 * A_ONE, a_first, 0)
-        a_join(1, 3).wait_recv()
-        lax.fori_loop(2 * A_ONE, A_TURN, a_first, 0)
+    def b_first(g, s):
+        def step(m, carry):
+            for k in range(4):
+                b_half(g, s, 4 * m + k, k).start()
+            return carry
+
+        lax.fori_loop(0, NBC // 4, step, 0)
+
+    def a_first(s):
+        def step(k, carry):
+            for back in range(2):
+                a_half(s, a_chunk(k, back), back).start()
+            return carry
+
+        lax.fori_loop(0, A_TURN, step, 0)
+        a_join(s).start()
+
+    each_source(lambda s: None, b_first)
+    each_source(a_first, lambda g, s: None)
 
     top = core1 & (p == 0)
     edge = core1 & (y == 0)
@@ -337,7 +343,14 @@
 
                 @pl.when((m >= 0) & (m < A_TURN) & a_comes(k, back))
                 def _():
-                    a_ring(n, back).wait_recv()
+                    @pl.when(a_hops[back] == 1)
+                    def _():
+                        for s in range(2):
+                            a_half(s, n, back).wait_recv()
+
+                    @pl.when(a_hops[back] != 1)
+                    def _():
+                        a_ring(n, back).wait_recv()
 
                     @pl.when(a_more(k, back))
                     def _():
@@ -356,7 +369,15 @@
 
                 @pl.when((p != s) & (m >= 0) & (m < NBC // 4))
                 def _():
-                    b_plane(s, n, k, 0).wait_recv()
+                    @pl.when(hops == 1)
+                    def _():
+                        for g in range(2):
+                            b_half(g, s, n, k).wait_recv()
+
+                    @pl.when(hops != 1)
+                    def _():
+                        b_plane(s, n, k, 0).wait_recv()
+
                     for way in range(4):
                         @pl.when(sends[way])
                         def _():
@@ -382,8 +403,7 @@
     def a_wait_sib():
         @pl.when(a_source)
         def _():
-            for i in range(4):
-                a_join(0, i).wait_recv()
+            a_join(0).wait_recv()
 
         @pl.when(jnp.logical_not(a_source))
         def _():
@@ -431,12 +451,17 @@
                     put(start, start + size, work[last - size : last, NB:])
 
         factor_inverse(work, strip)
+        a_wait_sib()
         b_wait_sib()
         a_store.start()
         b_store(0).start()
 
     @pl.when(core0 & jnp.logical_not(head))
     def _():
+        @pl.when(a_source)
+        def _():
+            a_wait_sib()
+
         a_store.start()
         b_wait_sib()
         b_store(0).start()
@@ -453,14 +478,16 @@
 
     f_store.start()
 
-    each_source(
-        lambda s: [a_join(s, i).wait_send() for i in range(4)],
-        lambda g, s: [b_join(s, i).wait_send() for i in range(4)] if g == 0 else None,
-    )
+    def a_given(s):
+        for back in range(2):
+            a_gave(s, back).wait_send()
+        a_join(s).wait_send()
+
+    each_source(a_given, lambda g, s: b_gave(g, s).wait_send())
 
     for back in range(2):
         for group, k in enumerate((0, A_ONE)):
-            @pl.when(core0 & (a_source | (a_comes(k, back) & a_more(k, back))))
+            @pl.when(core0 & (z != 0) & a_comes(k, back) & a_more(k, back))
             def _():
                 a_sent(back, group).wait_send()
 
@@ -470,9 +497,7 @@
 
     for (s, k), (hops, sends) in trees.items():
         for way in range(4):
-            mine = jnp.where(p == s, way == k, sends[way])
-
-            @pl.when(core1 & mine)
+            @pl.when(core1 & (p != s) & sends[way])
             def _():
                 b_sent(s, k, way).wait_send()
 
@@ -526,8 +551,10 @@
             pltpu.SemaphoreType.DMA((18,)),
             pltpu.SemaphoreType.DMA((2,)),
             pltpu.SemaphoreType.DMA((2,)),
-            pltpu.SemaphoreType.DMA((2, 4)),
-            pltpu.SemaphoreType.DMA((2, 4)),
+            pltpu.SemaphoreType.DMA,
+            pltpu.SemaphoreType.DMA((4,)),
+            pltpu.SemaphoreType.DMA((NA,)),
+            pltpu.SemaphoreType.DMA((2, NBC)),
             pltpu.SemaphoreType.DMA((2,)),
             pltpu.SemaphoreType.DMA((2,)),
             pltpu.SemaphoreType.DMA,
@@ -566,20 +593,24 @@
 
 def update_kernel(
     m_ref, noise_ref, a_ref, b_ref, f_ref, out_ref,
-    m_buf, a_buf, b_buf, f_buf, rows, cols, m_sem, a_sem, b_sem, f_sem, out_sem,
+    m_buf, a_buf, b_buf, f_buf, rows, cols, m_sem, a_sem, b_sem, f_sem, out_sem, up_sem,
 ):
     p, q = lax.axis_index("row"), lax.axis_index("col")
     strip = [pl.ds(t * NB, NB) for t in range(T)]
     f_load = pltpu.make_async_copy(f_ref, f_buf, f_sem)
     b_load = pltpu.make_async_copy(b_ref, b_buf, b_sem)
     a_load = pltpu.make_async_copy(a_ref, a_buf, a_sem)
-    m_load = [pltpu.make_async_copy(m_ref.at[strip[t]], m_buf.at[strip[t]], m_sem.at[t]) for t in range(T)]
-    store = [pltpu.make_async_copy(m_buf.at[strip[t]], out_ref.at[strip[t]], out_sem.at[t]) for t in range(T)]
+    lower = [(strip[t], pl.ds(0, (t + 1) * NB)) for t in range(T)]
+    upper = [(strip[t], pl.ds((t + 1) * NB, LOCAL - (t + 1) * NB)) for t in range(T - 1)]
+    m_load = [pltpu.make_async_copy(m_ref.at[lower[t]], m_buf.at[lower[t]], m_sem.at[t]) for t in range(T)]
+    store = [pltpu.make_async_copy(m_buf.at[lower[t]], out_ref.at[lower[t]], out_sem.at[t]) for t in range(T)]
+    u_load = [pltpu.make_async_copy(m_ref.at[upper[t]], m_buf.at[upper[t]], up_sem.at[0, t]) for t in range(T - 1)]
+    u_store = [pltpu.make_async_copy(m_buf.at[upper[t]], out_ref.at[upper[t]], up_sem.at[1, t]) for t in range(T - 1)]
     f_load.start()
     a_load.start()
     b_load.start()
-    for t in range(T):
-        m_load[t].start()
+    for copy in u_load + m_load:
+        copy.start()
 
     f_load.wait()
     x0, l10, x1 = [split(f_buf[k * NB : (k + 1) * NB, :]) for k in range(3)]
@@ -590,6 +621,9 @@
     row1_parts = split(row1)
     for at, value in enumerate((row0_parts[0], row1_parts[0], row0_parts[1], row1_parts[1])):
         rows[:, at * NB : (at + 1) * NB] = value
+    for load, copy in zip(u_load, u_store):
+        load.wait()
+        copy.start()
     b_load.wait()
     col0 = split(product(left(x0), below(split(b_buf[0]))))
     col1 = split(product(left(x1), below(split(b_buf[1] - product(left(l10), below(col0))))))
@@ -626,8 +660,8 @@
                 m_buf[NB:, at] = panel[NB:]
 
         store[col].start()
-    for t in range(T):
-        store[t].wait()
+    for copy in store + u_store:
+        copy.wait()
 
 
 def update(kernel, noise, a, b, f):
@@ -649,6 +683,7 @@
             pltpu.SemaphoreType.DMA,
             pltpu.SemaphoreType.DMA,
             pltpu.SemaphoreType.DMA((T,)),
+            pltpu.SemaphoreType.DMA((2, T - 1)),
         ],
         compiler_params=pltpu.CompilerParams(vmem_limit_bytes=48 * 2**20),
         name="update",

time: 67.5 us -> 64 us (0.948)
  Pallas kernels: 66.4 us -> 63 us
    pallas_call x1, Pallas kernels: 55.4 us -> 52.3 us  [gather(): pl.pallas_call(gather_kernel, out_shape=(jax.ShapeDtypeStruct((LOCAL, 2 *...]
where the time goes in v6:
time: 64 us; the launch traced here: 63.8 us
  Pallas kernels  63 us (98%)
  local copies, waits for them, and re-layouts  0.7 us (1%)
    pallas_call x1, Pallas kernels, gather(): pl.pallas_call(gather_kernel, out_shape=(jax.ShapeDtypeStruct((LOCAL, 2 *...  52.3 us
    pallas_call x1, Pallas kernels, update(): pl.pallas_call(update_kernel, out_shape=jax.ShapeDtypeStruct((LOCAL, LOCA...  10.7 us

profile of v6, /device:TPU:141, one launch (start us, length us, event | category | flops | bytes accessed | tf_op | source)
XLA Modules:
  0.0 63.8 jit_solution(9289075290718748770)
XLA Ops:
  0.0 0.7 %reshape.3.noise_ref = f32[1,1280]{1,0:T(1,128)S(1)} reshape(f32[1280]{0:T(1024)} %param.3) | data formatting | bytes 10240 | tf_op jit(solution)/shard_map/reshape | solution.py:694
  0.7 52.3 %gather_factor.1 = (f32[1280,512]{1,0:T(8,128)S(1)}, f32[2,256,1280]{2,1,0:T(8,128)S(1)}, f32[768,256]{1,0:T(8,128)S(1)}) custom-call(f32[1280,1280]{1,0:T(8,128)} %m_ref.1, f32[1,1280]{1,0:T(1,128)S(1)} %reshape.3.noise_ref), custom_call_target="tpu_custom_call" | custom-call | tf_op jit(solution)/shard_map/gather_factor/pallas_call | solution.py:529
  53.0 10.7 %update.1 = f32[1280,1280]{1,0:T(8,128)} custom-call(f32[1280,1280]{1,0:T(8,128)} %m_ref.1, f32[1,1280]{1,0:T(1,128)S(1)} %reshape.3.noise_ref, f32[1280,512]{1,0:T(8,128)S(1)} %get-tuple-element.8.a_ref, f32[2,256,1280]{2,1,0:T(8,128)S(1)} %get-tuple-element.9.b_ref, f32[768,256]{1,0:T(8,128)S(1)} %get-tuple-element.10.f_ref), custom_call_target="tpu_custom_call" | custom-call | tf_op jit(solution)/shard_map/update/pallas_call | solution.py:669

commit v7 on v6

--- a/solution.py
+++ b/solution.py
@@ -26,11 +26,11 @@
 F_SLOT = 3
 B_SLOTS = max(9, F_SLOT + 8)
 PIECES = (
-    ((0, 64, 128), (64, 64, 128), (128, 64, 256), (192, 64, 256))
-    + tuple((NB + 64 * n, 64, 256) for n in range(4))
+    ((0, 64, 128), (64, 64, 128), (128, 32, 256), (160, 32, 256), (192, 32, 256), (224, 32, 256))
+    + tuple((NB + 32 * n, 32, 256) for n in range(8))
     + ((512, 64, 128), (576, 64, 128), (640, 64, 256), (704, 32, 256), (736, 32, 256))
 )
-STRIPS = 8
+STRIPS = 14
 NF = len(PIECES)
 
 

time: 64 us -> 62.8 us (0.981); the launches traced: 63.8 us -> 61.9 us
  Pallas kernels: 63 us -> 61.1 us
    pallas_call x1, Pallas kernels: 52.3 us -> 50.4 us  [gather(): pl.pallas_call(gather_kernel, out_shape=(jax.ShapeDtypeStruct((LOCAL, 2 *...]
where the time goes in v7:
time: 62.8 us; the launch traced here: 61.9 us
  Pallas kernels  61.1 us (97%)
  local copies, waits for them, and re-layouts  0.7 us (1%)
    pallas_call x1, Pallas kernels, gather(): pl.pallas_call(gather_kernel, out_shape=(jax.ShapeDtypeStruct((LOCAL, 2 *...  50.4 us
    pallas_call x1, Pallas kernels, update(): pl.pallas_call(update_kernel, out_shape=jax.ShapeDtypeStruct((LOCAL, LOCA...  10.7 us

profile of v7, /device:TPU:141, one launch (start us, length us, event | category | flops | bytes accessed | tf_op | source)
XLA Modules:
  0.0 61.9 jit_solution(17559693083353035324)
XLA Ops:
  0.0 0.7 %reshape.3.noise_ref = f32[1,1280]{1,0:T(1,128)S(1)} reshape(f32[1280]{0:T(1024)} %param.3) | data formatting | bytes 10240 | tf_op jit(solution)/shard_map/reshape | solution.py:694
  0.7 50.4 %gather_factor.1 = (f32[1280,512]{1,0:T(8,128)S(1)}, f32[2,256,1280]{2,1,0:T(8,128)S(1)}, f32[768,256]{1,0:T(8,128)S(1)}) custom-call(f32[1280,1280]{1,0:T(8,128)} %m_ref.1, f32[1,1280]{1,0:T(1,128)S(1)} %reshape.3.noise_ref), custom_call_target="tpu_custom_call" | custom-call | tf_op jit(solution)/shard_map/gather_factor/pallas_call | solution.py:529
  51.1 10.7 %update.1 = f32[1280,1280]{1,0:T(8,128)} custom-call(f32[1280,1280]{1,0:T(8,128)} %m_ref.1, f32[1,1280]{1,0:T(1,128)S(1)} %reshape.3.noise_ref, f32[1280,512]{1,0:T(8,128)S(1)} %get-tuple-element.8.a_ref, f32[2,256,1280]{2,1,0:T(8,128)S(1)} %get-tuple-element.9.b_ref, f32[768,256]{1,0:T(8,128)S(1)} %get-tuple-element.10.f_ref), custom_call_target="tpu_custom_call" | custom-call | tf_op jit(solution)/shard_map/update/pallas_call | solution.py:669
